TPU v7x, 512 devices: a whole 4x4x16 slice. The times are simulated.
512 devices in a mesh: seq: 64 (over y, z), batch: 8 (over x, core).
Axes of the slice: x: 4, y: 4, z: 16, core: 2. Of those that a mesh axis runs over, the one named last changes fastest.
Arguments:
- queries: bfloat16 [8, 8192, 2048], P('batch', 'seq'), may hold values from -6 to 6
- out_grad: bfloat16 [8, 8192, 2048], P('batch', 'seq'), may hold values from -6 to 6
- states: bfloat16 [8, 1024, 8, 896], P('batch', 'seq'), may hold values from -6 to 6
- gain: float32 [896], replicated, may hold values from 0.25 to 1.75
- kv_weight: bfloat16 [896, 2, 2048], P('batch'), may hold values from -0.1875 to 0.1875
- owners: int32 [8, 128, 8], P('batch', 'seq'), may hold values from 0 to 63, all different within a row; in each aligned block of 2 rows (0 to 1, 2 to 3, ..., all dimensions but the last counted through in order) at most 2 rows name the same one
- slots: int32 [8, 128, 8], P('batch', 'seq'), may hold values from 0 to 15
Outputs:
- query_grad: bfloat16 [8, 8192, 2048], P('batch', 'seq')
- state_grad: bfloat16 [8, 1024, 8, 896], P('batch', 'seq')
- gain_grad: float32 [896], replicated
Inputs may be any that keep to these rules, and one draw needn't show every extreme that they name: `owners`: the 8 entries of a group differ; in each aligned block of 2 groups (the groups of one device) no shard is named more than 2 times, and some block names one exactly 2 times.
All inputs are finite; a program needn't handle non-finite values.
Results may differ from a plain program's by a relative error of at most 0.0089.
Values may be sent and summed in bfloat16 or wider, within the bound.
A program may use at most 128 MiB of HBM per device.

v0:
```python
import math

import jax
import jax.numpy as jnp
from jax import lax
from jax.sharding import PartitionSpec as P

HEADS = 16
HEAD_DIM = 128
GROUP = 64


EPS = 1e-06


def passed_along(x, axis, by):
    length = lax.axis_size(axis)
    pairs = [(i, i + by) for i in range(length) if 0 <= i + by < length]
    return lax.ppermute(x, axis, pairs)


def block_backward(query_block, grad_block, key_block, value_block):
    scaling = 1.0 / math.sqrt(query_block.shape[-1])
    scores = (
        jnp.einsum("uqhe,ukhe->uhqk", query_block, key_block, preferred_element_type=jnp.float32)
        * scaling
    )
    weights = jnp.exp(scores)
    probability = weights / jnp.sum(weights, axis=-1, keepdims=True)
    probability_low = probability.astype(jnp.bfloat16)
    grad_probability = jnp.einsum(
        "uqhe,ukhe->uhqk", grad_block, value_block, preferred_element_type=jnp.float32
    )
    delta_sum = jnp.sum(probability * grad_probability, axis=-1, keepdims=True)
    grad_scores = (probability * (grad_probability - delta_sum) * scaling).astype(jnp.bfloat16)
    query_grad = jnp.einsum(
        "uhqk,ukhe->uqhe", grad_scores, key_block, preferred_element_type=jnp.float32
    )
    key_next = jnp.einsum(
        "uhqk,uqhe->ukhe",
        grad_scores[:, :, 1:],
        query_block[:, 1:],
        preferred_element_type=jnp.float32,
    )
    value_next = jnp.einsum(
        "uhqk,uqhe->ukhe",
        probability_low[:, :, 1:],
        grad_block[:, 1:],
        preferred_element_type=jnp.float32,
    )
    return (query_grad, key_next, value_next, grad_scores[:, :, 0], probability_low[:, :, 0])


def self_term(query_first, grad_first, score_first, weight_first, split_weight):
    highest = lax.Precision.HIGHEST
    firsts = jnp.stack([query_first, grad_first], axis=1)
    maps = jnp.einsum("ushe,fshe->ushf", firsts, split_weight, preferred_element_type=jnp.float32)
    first = jnp.einsum(
        "uhk,uhf->ukf", score_first.astype(jnp.float32), maps[:, 0], precision=highest
    )
    second = jnp.einsum(
        "uhk,uhf->ukf", weight_first.astype(jnp.float32), maps[:, 1], precision=highest
    )
    return first + second


def on_device(queries, out_grad, states, gain, kv_weight, owners, slots):
    peer_count = lax.axis_size("seq")
    token_count = queries.shape[1]
    width = queries.shape[2]
    group_count = owners.shape[1]
    per_group = owners.shape[2]
    request_count = group_count * per_group
    capacity = max(2, -(-request_count // peer_count))
    slot_count = peer_count * capacity
    held = states.shape[1]
    length = states.shape[2]
    enc_width = states.shape[3]
    values = states[0].astype(jnp.float32)
    inverse = lax.rsqrt(jnp.mean(values * values, axis=-1, keepdims=True) + EPS)
    normed = (values * inverse * gain).astype(jnp.bfloat16).reshape(held, length * enc_width)
    targets = owners[0].reshape(-1)
    slot_ids = slots[0].reshape(-1)
    ranking = jnp.arange(request_count, dtype=jnp.int32)
    earlier = (targets[None, :] == targets[:, None]) & (ranking[None, :] < ranking[:, None])
    positions = jnp.sum(earlier.astype(jnp.int32), axis=1)
    columns = targets * capacity + positions
    placing_mask = columns[:, None] == jnp.arange(slot_count, dtype=jnp.int32)[None, :]
    placing = placing_mask.astype(jnp.bfloat16)
    wanted = jnp.sum(jnp.where(placing_mask, slot_ids[:, None] + 1, 0), axis=0) - 1
    asked = lax.all_to_all(
        wanted.reshape(peer_count, capacity), "seq", split_axis=0, concat_axis=0, tiled=True
    )
    select = (asked.reshape(-1)[:, None] == jnp.arange(held, dtype=jnp.int32)[None, :]).astype(
        jnp.bfloat16
    )
    replies = jnp.dot(select, normed, preferred_element_type=jnp.float32).astype(jnp.bfloat16)
    received = lax.all_to_all(
        replies.reshape(peer_count, capacity, length * enc_width),
        "seq",
        split_axis=0,
        concat_axis=0,
        tiled=True,
    )
    mine_rows = jnp.dot(
        placing,
        received.reshape(slot_count, length * enc_width),
        preferred_element_type=jnp.float32,
    ).astype(jnp.bfloat16)
    gathered = lax.all_gather(kv_weight, "batch", axis=0, tiled=True)
    flat_weight = gathered.reshape(enc_width, 2 * width)
    split_weight = gathered.reshape(enc_width, 2, HEADS, HEAD_DIM)
    previous = passed_along(mine_rows[request_count - per_group :], "seq", 1)
    result = jnp.dot(
        jnp.concatenate([previous, mine_rows], axis=0).reshape(-1, enc_width),
        flat_weight,
        preferred_element_type=jnp.float32,
    )
    pairs = result.astype(jnp.bfloat16).reshape(-1, length, 2, width)
    pairs = pairs.reshape(group_count + 1, per_group * length, 2, HEADS, HEAD_DIM)
    leading = jnp.zeros((1, width), jnp.bfloat16)
    trailing = jnp.zeros((GROUP - 1, width), jnp.bfloat16)
    query_block = jnp.concatenate([leading, queries[0], trailing], axis=0).reshape(
        group_count + 1, GROUP, HEADS, HEAD_DIM
    )
    grad_block = jnp.concatenate([leading, out_grad[0], trailing], axis=0).reshape(
        group_count + 1, GROUP, HEADS, HEAD_DIM
    )
    query_grad, key_next, value_next, score_first, weight_first = block_backward(
        query_block, grad_block, pairs[:, :, 0], pairs[:, :, 1]
    )
    query_grad = query_grad.reshape(-1, width)[1 : token_count + 1].astype(jnp.bfloat16)
    next_pairs = jnp.stack([key_next, value_next], axis=2).astype(jnp.bfloat16)
    next_pairs = next_pairs.reshape(group_count + 1, per_group * length, 2 * width)
    own_self = self_term(
        query_block[1:, 0], grad_block[1:, 0], score_first[1:], weight_first[1:], split_weight
    )
    returned = passed_along(next_pairs[0], "seq", -1)
    own_next = jnp.concatenate([next_pairs[1:group_count], returned[None]], axis=0)
    flat = own_next.reshape(-1, own_next.shape[-1])
    result = lax.dot_general(
        flat, flat_weight, (((1,), (1,)), ((), ())), preferred_element_type=jnp.float32
    )
    row_grad = result.reshape(own_next.shape[:-1] + (enc_width,)) + own_self
    row_grad = row_grad.astype(jnp.bfloat16).reshape(request_count, length * enc_width)
    outgoing = lax.dot_general(
        placing, row_grad, (((0,), (0,)), ((), ())), preferred_element_type=jnp.float32
    ).astype(jnp.bfloat16)
    incoming = lax.all_to_all(
        outgoing.reshape(peer_count, capacity, length * enc_width),
        "seq",
        split_axis=0,
        concat_axis=0,
        tiled=True,
    )
    normed_grad = lax.dot_general(
        select,
        incoming.reshape(slot_count, length * enc_width),
        (((0,), (0,)), ((), ())),
        preferred_element_type=jnp.float32,
    )
    normed_grad = normed_grad.reshape(held, length, enc_width)
    scaled = normed_grad * gain
    state_grad = (
        inverse * scaled
        - values * inverse * inverse * inverse * jnp.mean(scaled * values, axis=-1, keepdims=True)
    ).astype(jnp.bfloat16)
    gain_grad = lax.psum(jnp.sum(normed_grad * values * inverse, axis=(0, 1)), ("seq", "batch"))
    return (query_grad[None], state_grad[None], gain_grad)


def solution(mesh):
    return jax.shard_map(
        on_device,
        mesh=mesh,
        in_specs=(
            P("batch", "seq", None),
            P("batch", "seq", None),
            P("batch", "seq", None, None),
            P(),
            P("batch", None, None),
            P("batch", "seq", None),
            P("batch", "seq", None),
        ),
        out_specs=(P("batch", "seq", None), P("batch", "seq", None, None), P()),
        check_vma=False,
    )
```

profile of v0, /device:TPU:6, one launch (start us, length us, event | category | flops | bytes accessed | tf_op | source)
XLA Modules:
  0.0 440.4 jit_solution(12787946021263968501)
XLA Ops:
  7.2 0.7 all-gather.2.cloned.1.call-update
  7.9 0.7 broadcast_add_fusion
  8.7 0.8 reshape_squeeze.3
  9.4 0.2 convert_reduce_fusion
  9.7 0.8 sub.18
  10.5 18.7 %all-to-all-start = ((s32[64,1,2]{2,1,0:T(1,128)}), s32[64,1,2]{2,1,0:T(1,128)S(1)}, u32[]{:S(2)}, u32[]{:S(2)}) async-start(s32[64,1,2]{2,1,0:T(1,128)} %bitcast), calls=%async_computation | async-start | bytes 65536 | tf_op jit(solution)/shard_map/all_to_all | solution.py:91
  29.2 1.1 fusion.17
  30.3 1.0 fusion.57
  31.7 11.9 %all-to-all-done = s32[64,1,2]{2,1,0:T(1,128)S(1)} async-done(((s32[64,1,2]{2,1,0:T(1,128)}), s32[64,1,2]{2,1,0:T(1,128)S(1)}, u32[]{:S(2)}, u32[]{:S(2)}) %all-to-all-start) | async-done | bytes 544 | tf_op jit(solution)/shard_map/all_to_all | solution.py:91
  43.6 0.5 broadcast.82
  44.1 0.7 reduce.3
  44.9 0.7 convolution_convert_fusion.1
  45.6 1.7 reshape.112
  47.3 4.7 %all-to-all-start.1 = ((bf16[64,2,7168]{2,1,0:T(2,128)(2,1)}), bf16[64,2,7168]{2,1,0:T(2,128)(2,1)S(1)}, u32[]{:S(2)}, u32[]{:S(2)}) async-start(bf16[64,2,7168]{2,1,0:T(2,128)(2,1)} %reshape.112), calls=%async_computation.1 | async-start | bytes 3670016 | tf_op jit(solution)/shard_map/all_to_all | solution.py:98
  52.1 85.9 %all-to-all-done.1 = bf16[64,2,7168]{2,1,0:T(2,128)(2,1)S(1)} async-done(((bf16[64,2,7168]{2,1,0:T(2,128)(2,1)}), bf16[64,2,7168]{2,1,0:T(2,128)(2,1)S(1)}, u32[]{:S(2)}, u32[]{:S(2)}) %all-to-all-start.1) | async-done | bytes 1835040 | tf_op jit(solution)/shard_map/all_to_all | solution.py:98
  138.0 1.7 reshape.113
  139.7 2.0 convolution_convert_fusion.2
  141.7 3.4 collective-permute-start
  145.1 0.5 maximum_bitcast_fusion
  145.6 0.2 copy.104
  145.8 1.2 copy.73
  147.0 0.2 copy.99
  147.1 1.1 copy.71
  148.3 0.2 reshape.114
  148.5 7.8 %copy.102 = bf16[112,8,2,2048]{3,1,2,0:T(8,128)(2,1)S(1)} copy(bf16[112,8,2,2048]{3,2,1,0:T(2,128)(2,1)} %bitcast.111) | data formatting | bytes 14680064
  156.3 1.8 fusion.4
  158.1 0.3 copy.103
  158.4 0.3 fusion.55
  158.7 0.5 fusion.16
  159.3 0.3 copy-done.1
  159.6 0.7 fusion.56
  160.3 0.5 fusion.54
  160.8 16.9 %multiply_convert_fusion = bf16[3,16,64,64]{3,2,1,0:T(8,128)(2,1)S(1)} fusion(f32[3,16,64,64]{3,2,1,0:T(8,128)S(1)} %fusion.16, f32[3,16,64,64]{3,2,1,0:T(8,128)S(1)} %get-tuple-element.26, f32[3,16,64]{2,1,0:T(8,128)S(1)} %get-tuple-element.25), kind=kOutput, calls=%fused_computation.5 | output fusion | flops 1379391 | bytes 1978368 | tf_op jit(solution)/shard_map/sub | solution.py:35
  177.8 0.6 fusion.6
  178.4 0.8 copy-done.5
  179.2 0.6 fusion.5
  179.9 0.3 copy.80
  180.2 1.0 squeeze.28
  181.2 1.3 collective-permute-start.1
  182.5 18.8 %copy.83 = bf16[896,2,2048]{0,2,1:T(8,128)(2,1)} copy(bf16[896,2,2048]{2,1,0:T(2,128)(2,1)} %all-gather.2.cloned.1.call-done) | data formatting | bytes 14680064 | tf_op jit(solution)/shard_map/all_gather | solution.py:110
  201.3 4.3 convolution_bitcast_fusion
  205.7 0.9 slice.90
  206.5 0.9 slice.94
  207.4 0.3 copy.79
  207.7 0.2 slice.72
  208.0 12.8 %reshape.125 = bf16[896,4096,1]{1,0,2:T(8,128)(2,1)} reshape(bf16[896,2,2048]{2,1,0:T(2,128)(2,1)} %all-gather.2.cloned.1.call-done) | data formatting | bytes 14680064 | tf_op jit(solution)/shard_map/reshape | solution.py:111
  220.7 0.4 fusion.29
  221.1 0.4 convolution_add_fusion
  221.5 5.5 %fusion.8 = bf16[2,64,896]{2,1,0:T(8,128)(2,1)S(1)} fusion(f32[2,64,896]{2,1,0:T(8,128)S(1)} %convolution_add_fusion, bf16[896,4096,1]{1,0,2:T(8,128)(2,1)} %reshape.125, bf16[1,64,4096]{2,1,0:T(8,128)(2,1)S(1)} %bitcast.129, bf16[1,64,4096]{2,1,0:T(8,128)(2,1)S(1)} %slice.72), kind=kOutput, calls=%fused_computation.18 | convolution fusion | flops 940277760 | bytes 9076736 | tf_op jit(solution)/shard_map/dot_general | solution.py:141
  227.0 0.8 reshape.120
  227.8 1.7 convolution_convert_fusion
  229.5 1.7 reshape.121
  231.2 10.4 %all-to-all-start.2 = ((bf16[64,2,7168]{2,1,0:T(2,128)(2,1)}), bf16[64,2,7168]{2,1,0:T(2,128)(2,1)S(1)}, u32[]{:S(2)}, u32[]{:S(2)}) async-start(bf16[64,2,7168]{2,1,0:T(2,128)(2,1)} %reshape.121), calls=%async_computation.2 | async-start | bytes 3670016 | tf_op jit(solution)/shard_map/all_to_all | solution.py:149
  241.6 19.9 %fusion.7 = bf16[3,64,16,128]{3,1,2,0:T(8,128)(2,1)} fusion(bf16[3,64,1,16,128]{4,3,2,1,0:T(8,128)(2,1)} %copy-done.1, f32[3,16,64,64]{3,2,1,0:T(8,128)} %copy-done.2, f32[3,16,64,64]{3,2,1,0:T(8,128)S(1)} %get-tuple-element.26, f32[3,16,64]{2,1,0:T(8,128)S(1)} %get-tuple-element.25), kind=kOutput, calls=%fused_computation.15 | convolution fusion | flops 52104256 | bytes 3158016 | tf_op jit(solution)/shard_map/uhqk,ukhe->uqhe/dot_general | solution.py:36
  261.5 1.6 copy.74
  263.1 0.2 copy.140
  263.4 0.9 slice_bitcast_fusion
  264.3 62.9 %all-to-all-done.2 = bf16[64,2,7168]{2,1,0:T(2,128)(2,1)S(1)} async-done(((bf16[64,2,7168]{2,1,0:T(2,128)(2,1)}), bf16[64,2,7168]{2,1,0:T(2,128)(2,1)S(1)}, u32[]{:S(2)}, u32[]{:S(2)}) %all-to-all-start.2) | async-done | bytes 1835040 | tf_op jit(solution)/shard_map/all_to_all | solution.py:149
  327.2 1.7 reshape.122
  328.9 3.3 copy.87
  332.2 0.7 fusion.25
  332.9 0.2 fusion.26
  333.1 0.7 copy.88
  333.8 99.7 %psum.7 = f32[896]{0:T(1024)} all-reduce(f32[896]{0:T(1024)S(1)} %get-tuple-element.15), channel_id=1, replica_groups=mesh['seq'=64,'batch'=8] {'seq','batch'}, use_global_device_ids=true, to_apply=%region_7.8 | all-reduce | flops 896 | bytes 7168 | tf_op jit(solution)/shard_map/psum | solution.py:168
  (46 shorter events, 1.0 us)
Async XLA Ops:
  7.2 141.3 %all-gather.2.cloned.1.call-start = ((), (), s32[]{:S(2)}) async-start(), calls=%async_computation.3 | async-start | bytes 8257536 | tf_op jit(solution)/shard_map/all_gather | solution.py:110
  10.5 33.1 %all-to-all-start = ((s32[64,1,2]{2,1,0:T(1,128)}), s32[64,1,2]{2,1,0:T(1,128)S(1)}, u32[]{:S(2)}, u32[]{:S(2)}) async-start(s32[64,1,2]{2,1,0:T(1,128)} %bitcast), calls=%async_computation | async-start | bytes 65536 | tf_op jit(solution)/shard_map/all_to_all | solution.py:91
  29.2 2.4 copy-start.8
  47.3 90.7 %all-to-all-start.1 = ((bf16[64,2,7168]{2,1,0:T(2,128)(2,1)}), bf16[64,2,7168]{2,1,0:T(2,128)(2,1)S(1)}, u32[]{:S(2)}, u32[]{:S(2)}) async-start(bf16[64,2,7168]{2,1,0:T(2,128)(2,1)} %reshape.112), calls=%async_computation.1 | async-start | bytes 3670016 | tf_op jit(solution)/shard_map/all_to_all | solution.py:98
  139.7 5.4 %copy-start.6 = (bf16[1,128,2048]{2,1,0:T(8,128)(2,1)S(1)}, bf16[1,128,2048]{2,1,0:T(8,128)(2,1)}, u32[]{:S(2)}) copy-start(bf16[1,128,2048]{2,1,0:T(8,128)(2,1)} %param.7) | copy-start | bytes 1572868
  139.7 5.4 %copy-start.7 = (bf16[1,128,2048]{2,1,0:T(8,128)(2,1)S(1)}, bf16[1,128,2048]{2,1,0:T(8,128)(2,1)}, u32[]{:S(2)}) copy-start(bf16[1,128,2048]{2,1,0:T(8,128)(2,1)} %param.8) | copy-start | bytes 1572868
  141.7 6.5 %collective-permute-start = (bf16[8,7168]{1,0:T(8,128)(2,1)S(1)}, bf16[8,7168]{1,0:T(8,128)(2,1)S(1)}, u32[]{:S(2)}, u32[]{:S(2)}) collective-permute-start(bf16[8,7168]{1,0:T(8,128)(2,1)S(1)} %slice.82), channel_id=1, source_target_pairs={{0,8},{8,16},{16,24},{24,32},{32,40},{40,48},{48,56},{56,64},{64,7... | collective-permute-start | bytes 344072 | tf_op jit(solution)/shard_map/ppermute | solution.py:19
  158.7 0.9 copy-start.1
  159.3 1.5 copy-start.2
  160.8 17.0 %copy-start.3 = (bf16[3,16,64,64]{3,2,1,0:T(8,128)(2,1)}, bf16[3,16,64,64]{3,2,1,0:T(8,128)(2,1)S(1)}, u32[]{:S(2)}) copy-start(bf16[3,16,64,64]{3,2,1,0:T(8,128)(2,1)S(1)} %fusion.54) | copy-start | bytes 1179652
  160.8 17.0 %copy-start.4 = (bf16[3,64,16,128]{3,1,2,0:T(8,128)(2,1)S(1)}, bf16[3,64,16,128]{3,1,2,0:T(8,128)(2,1)}, u32[]{:S(2)}) copy-start(bf16[3,64,16,128]{3,1,2,0:T(8,128)(2,1)} %copy.73) | copy-start | bytes 2359300
  177.8 2.0 copy-start.9
  177.8 1.4 copy-start.5
  181.2 40.2 %collective-permute-start.1 = (bf16[64,4096]{1,0:T(8,128)(2,1)}, bf16[64,4096]{1,0:T(8,128)(2,1)S(1)}, u32[]{:S(2)}, u32[]{:S(2)}) collective-permute-start(bf16[64,4096]{1,0:T(8,128)(2,1)} %squeeze.28), channel_id=1, source_target_pairs={{8,0},{16,8},{24,16},{32,24},{40,32},{48,40},{56,48},{64,56},{72,6... | collective-permute-start | bytes 1572872 | tf_op jit(solution)/shard_map/ppermute | solution.py:19
  231.2 96.0 %all-to-all-start.2 = ((bf16[64,2,7168]{2,1,0:T(2,128)(2,1)}), bf16[64,2,7168]{2,1,0:T(2,128)(2,1)S(1)}, u32[]{:S(2)}, u32[]{:S(2)}) async-start(bf16[64,2,7168]{2,1,0:T(2,128)(2,1)} %reshape.121), calls=%async_computation.2 | async-start | bytes 3670016 | tf_op jit(solution)/shard_map/all_to_all | solution.py:149
  328.9 3.3 copy-start
Sparse Core Ops, SparseCore 0:
  10.1 55.5 all-gather.1
where the time goes:
time: 443 us; the launch traced here: 440 us
  waiting for transfers between devices  161 us (36%)
  blocking collectives  99.7 us (23%)
  local copies, waits for them, and re-layouts  64.6 us (15%)
  matrix products  39.6 us (9%)
  starting transfers between devices  38.5 us (9%)
  other arithmetic  22 us (5%)
  between operations  14.5 us (3%)
    psum x1, blocking collectives, on_device(): lax.psum(jnp.sum(normed_grad * values * inverse, axis=(0, 1)), ('seq', 'b...  99.7 us
    all_to_all x1, waiting for transfers between devices, on_device(): lax.all_to_all(replies.reshape(peer_count, capacity, length * enc_width),...  85.9 us
    all_to_all x1, waiting for transfers between devices, on_device(): lax.all_to_all(outgoing.reshape(peer_count, capacity, length * enc_width)...  62.9 us
    dot_general x1, matrix products, block_backward(): jnp.einsum('uhqk,ukhe->uqhe', grad_scores, key_block, preferred_element_t...  19.9 us
    all_gather x1, local copies, waits for them, and re-layouts, on_device(): gathered = lax.all_gather(kv_weight, 'batch', axis=0, tiled=True)  18.8 us
    all_to_all x1, starting transfers between devices, on_device(): lax.all_to_all(wanted.reshape(peer_count, capacity), 'seq', split_axis=0,...  18.7 us
    sub x1, other arithmetic, block_backward(): grad_probability - delta_sum  16.9 us
    reshape x1, local copies, waits for them, and re-layouts, on_device(): flat_weight = gathered.reshape(enc_width, 2 * width)  12.8 us
  transfers between devices with their start and end apart: 6, of which 3 were waited for; matrix products, arithmetic and copies ran while one was open for 18% of the time, Pallas kernels for 0%

commit v1 on v0

v1 whole, which is shorter than its diff:
```python
import functools
import math

import jax
import jax.numpy as jnp
from jax import lax
from jax.experimental import pallas as pl
from jax.experimental.pallas import tpu as pltpu
from jax.sharding import PartitionSpec as P

HEAD_DIM = 128
GROUP = 64
EPS = 1e-06
Y_SIZE = 4
CHUNKS = 2
CAP = 3

MESH = pl.DeviceIdType.MESH
VMEM = pltpu.VMEM
F32 = jnp.float32
BF16 = jnp.bfloat16


def one_hot(mask):
    return jnp.where(mask, 1.0, 0.0).astype(BF16)


class Place:
    def __init__(self, ny, nz):
        me = lax.axis_index("seq")
        self.ny, self.nz = ny, nz
        self.y = lax.div(me, nz)
        self.z = lax.rem(me, nz)
        self.up = self.at(self.y, lax.rem(self.z + 1, nz))
        self.down = self.at(self.y, lax.rem(self.z + nz - 1, nz))
        self.across = [lax.rem(self.y + j, ny) for j in range(1, ny)]

    def at(self, y, z):
        return {"seq": y * self.nz + z}


def greet(devices):
    barrier = pltpu.get_barrier_semaphore()
    for device in devices:
        pl.semaphore_signal(barrier, inc=1, device_id=device, device_id_type=MESH)
    pl.semaphore_wait(barrier, len(devices))


def remote(src, dst, send_sem, recv_sem, device):
    return pltpu.make_async_remote_copy(
        src_ref=src,
        dst_ref=dst,
        send_sem=send_sem,
        recv_sem=recv_sem,
        device_id=device,
        device_id_type=MESH,
    )


def fetch_kernel(
    ny, nz, states_ref, gain_ref, table_ref, pos_ref, mine_ref, tab_ref,
    ring, tabs, outs, recv, acc,
    ring_send, ring_recv, y_send, y_recv, tab_send, tab_recv,
):
    half = nz // 2
    place = Place(ny, nz)
    rows = states_ref.shape[0]
    part = rows // CHUNKS
    block = outs.shape[1] // ny
    y = place.y

    def ring_part(slot, way, chunk):
        return ring.at[slot, pl.ds(way * rows + chunk * part, part)]

    def forward(slot, way, chunk):
        far = isinstance(slot, int) and slot == half - 1
        first = isinstance(slot, int) and slot == 0
        src = ring_part(half - 1, 0, chunk) if first else ring_part(slot - 1, way, chunk)
        dst = ring_part(slot, 1, chunk) if far else ring_part(slot, way, chunk)
        return remote(
            src,
            dst,
            ring_send.at[slot, way, chunk],
            ring_recv.at[slot, way, chunk],
            place.down if way == 0 else place.up,
        )

    def across(slot, j):
        there = place.across[j]
        return remote(
            outs.at[slot, pl.ds(there * block, block)],
            recv.at[slot, pl.ds(y * block, block)],
            y_send.at[slot, j],
            y_recv.at[slot, j],
            place.at(there, place.z),
        )

    def table_copy(j):
        there = place.across[j]
        return remote(
            table_ref.at[there], tabs.at[y], tab_send.at[j], tab_recv.at[j], place.at(there, place.z)
        )

    values = states_ref[...].astype(F32)
    inverse = lax.rsqrt(jnp.mean(values * values, axis=-1, keepdims=True) + EPS)
    ring[half - 1, :rows] = (values * inverse * gain_ref[...]).astype(BF16)

    greet([place.up, place.down] + [place.at(there, place.z) for there in place.across])
    for chunk in range(CHUNKS):
        for way in range(2):
            forward(0, way, chunk).start()
    for j in range(ny - 1):
        table_copy(j).start()
    acc[...] = jnp.zeros_like(acc)
    tabs[pl.ds(y, 1)] = table_ref[pl.ds(y, 1)]
    for j in range(ny - 1):
        table_copy(j).wait()
    asked = tabs[0]
    for j in range(1, ny):
        asked = asked + tabs[j]
    tab_ref[...] = asked

    wide = outs.shape[1]

    def pick(slot):
        row = tab_ref[pl.ds(slot, 1), :wide]
        index = lax.broadcasted_iota(jnp.int32, (2 * rows, wide), 0) + 1
        select = one_hot(index == row)
        picked = lax.dot_general(
            select, ring[slot], (((0,), (0,)), ((), ())), preferred_element_type=F32
        ).astype(BF16)
        outs[slot] = picked
        for j in range(ny - 1):
            across(slot, j).start()
        recv[slot, pl.ds(y * block, block)] = outs[slot, pl.ds(y * block, block)]

    def take(slot):
        for j in range(ny - 1):
            across(slot, j).wait_recv()
        index = lax.broadcasted_iota(jnp.int32, (pos_ref.shape[0], wide), 1) + slot * wide
        placing = one_hot(index == pos_ref[...])
        acc[...] += jnp.dot(placing, recv[slot], preferred_element_type=F32)

    def near(slot, last):
        for chunk in range(CHUNKS):
            for way in range(2):
                forward(slot, way, chunk).wait_recv()
                if not last:
                    forward(slot + 1, way, chunk).start()
                elif way == chunk:
                    forward(half - 1, way, chunk).start()
        pick(slot)

    near(0, half == 2)
    if half > 2:

        @pl.loop(1, half - 2)
        def _(slot):
            near(slot, False)
            take(slot - 1)

        near(half - 2, True)
        take(half - 3)
    for way in range(2):
        forward(half - 1, way, way).wait_recv()
    pick(half - 1)
    take(half - 2)
    take(half - 1)
    mine_ref[...] = acc[...].astype(BF16)

    for way in range(2):
        forward(half - 1, way, way).wait_send()

    @pl.loop(0, half - 1)
    def _(slot):
        for way in range(2):
            for chunk in range(CHUNKS):
                remote(
                    ring_part(0, way, chunk),
                    ring_part(0, way, chunk),
                    ring_send.at[slot, way, chunk],
                    ring_recv.at[slot, way, chunk],
                    place.down if way == 0 else place.up,
                ).wait_send()

    @pl.loop(0, half)
    def _(slot):
        for j in range(ny - 1):
            across(slot, j).wait_send()


def fetch(ny, nz, states, gain, table, pos):
    half = nz // 2
    rows, width = states.shape
    wanted = pos.shape[0]
    block = 2 * CAP * 8
    return pl.pallas_call(
        functools.partial(fetch_kernel, ny, nz),
        out_shape=(
            jax.ShapeDtypeStruct((wanted, width), BF16),
            jax.ShapeDtypeStruct(table.shape[1:], jnp.int32),
        ),
        in_specs=[pl.BlockSpec(memory_space=VMEM)] * 4,
        out_specs=(pl.BlockSpec(memory_space=VMEM),) * 2,
        scratch_shapes=[
            VMEM((half, 2 * rows, width), BF16),
            VMEM(table.shape, jnp.int32),
            VMEM((half, ny * block, width), BF16),
            VMEM((half, ny * block, width), BF16),
            VMEM((wanted, width), F32),
            pltpu.SemaphoreType.DMA((half, 2, CHUNKS)),
            pltpu.SemaphoreType.DMA((half, 2, CHUNKS)),
            pltpu.SemaphoreType.DMA((half, ny - 1)),
            pltpu.SemaphoreType.DMA((half, ny - 1)),
            pltpu.SemaphoreType.DMA((ny - 1,)),
            pltpu.SemaphoreType.DMA((ny - 1,)),
        ],
        compiler_params=pltpu.CompilerParams(
            collective_id=1, has_side_effects=True, vmem_limit_bytes=40 << 20
        ),
        cost_estimate=pl.CostEstimate(flops=2 * 10**9, bytes_accessed=10**8, transcendentals=0),
    )(states, gain, table, pos)


def attend_kernel(
    pages_ref, group_ref, rgain_ref, q_ref, do_ref, wk_ref, wv_ref, dq_ref, grad_ref, gain_ref, acc
):
    step = pl.program_id(0)
    scaling = 1.0 / math.sqrt(HEAD_DIM)
    tokens, keys = q_ref.shape[0], pages_ref.shape[0]
    pages = pages_ref[...]
    key_all = jnp.dot(pages, wk_ref[...], preferred_element_type=F32).astype(BF16)
    value_all = jnp.dot(pages, wv_ref[...], preferred_element_type=F32).astype(BF16)
    mask = group_ref[...] == lax.div(lax.broadcasted_iota(jnp.int32, (tokens, keys), 1), GROUP)
    minor = (((1,), (1,)), ((), ()))
    major = (((0,), (0,)), ((), ()))
    key_grads, value_grads = [], []
    for head in range(q_ref.shape[1] // HEAD_DIM):
        columns = slice(head * HEAD_DIM, (head + 1) * HEAD_DIM)
        query, grad = q_ref[:, columns], do_ref[:, columns]
        key, value = key_all[:, columns], value_all[:, columns]
        scores = lax.dot_general(query, key, minor, preferred_element_type=F32) * scaling
        weights = jnp.where(mask, jnp.exp(jnp.where(mask, scores, 0.0)), 0.0)
        total = jnp.sum(weights, axis=-1, keepdims=True)
        probability = weights / jnp.where(total == 0.0, 1.0, total)
        grad_probability = lax.dot_general(grad, value, minor, preferred_element_type=F32)
        delta = jnp.sum(probability * grad_probability, axis=-1, keepdims=True)
        grad_scores = (probability * (grad_probability - delta) * scaling).astype(BF16)
        low = probability.astype(BF16)
        dq_ref[:, columns] = jnp.dot(grad_scores, key, preferred_element_type=F32).astype(BF16)
        key_grads.append(lax.dot_general(grad_scores, query, major, preferred_element_type=F32))
        value_grads.append(lax.dot_general(low, grad, major, preferred_element_type=F32))
    key_grad = jnp.concatenate(key_grads, axis=1).astype(BF16)
    value_grad = jnp.concatenate(value_grads, axis=1).astype(BF16)
    added = lax.dot_general(key_grad, wk_ref[...], minor, preferred_element_type=F32)
    added += lax.dot_general(value_grad, wv_ref[...], minor, preferred_element_type=F32)

    @pl.when(step == 0)
    def _():
        acc[...] = added

    @pl.when(step > 0)
    def _():
        acc[...] += added

    @pl.when(step == pl.num_programs(0) - 1)
    def _():
        picked_grad = acc[...].astype(BF16)
        grad_ref[...] = picked_grad
        products = picked_grad.astype(F32) * pages.astype(F32)
        gain_ref[...] = jnp.sum(products, axis=0, keepdims=True) * rgain_ref[...]


def attend(pages, group, rgain, queries, out_grad, weight):
    keys, enc = pages.shape
    tokens, width = queries.shape
    wide = 256
    steps = width // wide
    whole = lambda *shape: pl.BlockSpec(shape, lambda i: (0, 0))
    column = lambda rows, first: pl.BlockSpec((rows, wide), lambda i: (0, first + i))
    return pl.pallas_call(
        attend_kernel,
        grid=(steps,),
        out_shape=(
            jax.ShapeDtypeStruct((tokens, width), BF16),
            jax.ShapeDtypeStruct((keys, enc), BF16),
            jax.ShapeDtypeStruct((1, enc), F32),
        ),
        in_specs=[
            whole(keys, enc), whole(tokens, 1), whole(1, enc),
            column(tokens, 0), column(tokens, 0), column(enc, 0), column(enc, steps),
        ],
        out_specs=(column(tokens, 0), whole(keys, enc), whole(1, enc)),
        scratch_shapes=[VMEM((keys, enc), F32)],
        compiler_params=pltpu.CompilerParams(vmem_limit_bytes=32 << 20),
    )(pages, group, rgain, queries, out_grad, weight, weight)


def give_kernel(
    ny, nz, nb, grad_ref, pos_ref, tab_ref, states_ref, gain_ref, gain_part_ref, out_ref, gain_out_ref,
    outs, recv, sums_in, sums_out, added, own, by_batch, by_y, by_z,
    ring_send, ring_recv, y_send, y_recv, b_send, b_recv, gy_send, gy_recv, z_send, z_recv,
):
    half = nz // 2
    place = Place(ny, nz)
    y, z, b = place.y, place.z, lax.axis_index("batch")
    rows, width = states_ref.shape
    part = rows // CHUNKS
    wide = outs.shape[1]
    block = wide // ny
    b_peers = [lax.rem(b + j, nb) for j in range(1, nb)]
    z_peers = [lax.rem(z + j, nz) for j in range(1, nz)]

    def part_of(ref, slot, way, chunk):
        return ref.at[slot, pl.ds(way * rows + chunk * part, part)]

    def pass_on(distance, way, chunk):
        far = isinstance(distance, int) and distance == half
        return remote(
            part_of(sums_out, distance - 1, 1 if far else way, chunk),
            part_of(sums_in, distance - 1, way, chunk),
            ring_send.at[distance - 1, way, chunk],
            ring_recv.at[distance - 1, way, chunk],
            place.up if way == 0 else place.down,
        )

    def across(slot, j):
        there = place.across[j]
        return remote(
            outs.at[slot, pl.ds(there * block, block)],
            recv.at[slot, pl.ds(y * block, block)],
            y_send.at[slot, j],
            y_recv.at[slot, j],
            place.at(there, z),
        )

    def b_copy(j):
        return remote(
            by_batch.at[b], by_batch.at[b], b_send.at[j], b_recv.at[j], {"batch": b_peers[j]}
        )

    def gy_copy(j):
        return remote(
            by_y.at[y], by_y.at[y], gy_send.at[j], gy_recv.at[j], place.at(place.across[j], z)
        )

    def z_copy(j):
        return remote(
            by_z.at[z], by_z.at[z], z_send.at[j], z_recv.at[j], place.at(y, z_peers[j])
        )

    def total(ref):
        result = ref[0]
        for i in range(1, ref.shape[0]):
            result = result + ref[i]
        return result

    lanes = width // 128
    by_batch[pl.ds(b, 1)] = jnp.zeros_like(by_batch[pl.ds(b, 1)])
    for i in range(lanes):
        by_batch[b, i : i + 1] = gain_part_ref[:, i * 128 : (i + 1) * 128]

    greet(
        [{"batch": peer} for peer in b_peers]
        + [place.at(there, z) for there in place.across]
        + [place.at(y, there) for there in z_peers]
    )

    def scatter(slot):
        index = lax.broadcasted_iota(jnp.int32, (wide, pos_ref.shape[1]), 0) + slot * wide
        placing = one_hot(index == pos_ref[...])
        outs[slot] = jnp.dot(placing, grad_ref[...], preferred_element_type=F32).astype(BF16)
        for j in range(ny - 1):
            across(slot, j).start()
        recv[slot, pl.ds(y * block, block)] = outs[slot, pl.ds(y * block, block)]

    def gather(slot):
        for j in range(ny - 1):
            across(slot, j).wait_recv()
        row = tab_ref[pl.ds(slot, 1), :wide]
        index = lax.broadcasted_iota(jnp.int32, (2 * rows, wide), 0) + 1
        select = one_hot(index == row)
        added[...] = jnp.dot(select, recv[slot], preferred_element_type=F32)

    def chunk_rows(way, chunk):
        return pl.ds(way * rows + chunk * part, part)

    def relay(distance, first):
        gather(distance - 1)
        for chunk in range(CHUNKS):
            for way in range(2):
                here = chunk_rows(way, chunk)
                value = added[here]
                if not first or way == chunk:
                    pass_on(distance + 1, way, chunk).wait_recv()
                    value = value + sums_in[distance, here].astype(F32)
                sums_out[distance - 1, here] = value.astype(BF16)
                pass_on(distance, way, chunk).start()

    scatter(half - 1)
    for j in range(nb - 1):
        b_copy(j).start()
    if half > 1:
        scatter(half - 2)
    gather(half - 1)
    own[...] = added[:rows]
    sums_out[half - 1, pl.ds(rows, rows)] = added[pl.ds(rows, rows)].astype(BF16)
    for way in range(2):
        pass_on(half, way, way).start()
    if half > 2:
        scatter(half - 3)
    relay(half - 1, True)
    for j in range(nb - 1):
        b_copy(j).wait()
    by_y[y] = total(by_batch)
    for j in range(ny - 1):
        gy_copy(j).start()

    if half > 2:

        @pl.loop(0, half - 3)
        def _(i):
            distance = half - 2 - i
            scatter(distance - 2)
            relay(distance, False)

        for j in range(ny - 1):
            gy_copy(j).wait()
        by_z[z] = total(by_y)
        for j in range(nz - 1):
            z_copy(j).start()
        relay(1, False)
    else:
        for j in range(ny - 1):
            gy_copy(j).wait()
        by_z[z] = total(by_y)
        for j in range(nz - 1):
            z_copy(j).start()

    for j in range(nz - 1):
        z_copy(j).wait()
    result = total(by_z)
    for i in range(lanes):
        gain_out_ref[:, i * 128 : (i + 1) * 128] = result[i : i + 1]

    gain = gain_ref[...]
    for chunk in range(CHUNKS):
        here = pl.ds(chunk * part, part)
        for way in range(2):
            pass_on(1, way, chunk).wait_recv()
        normed_grad = own[here] + sums_in[0, here].astype(F32)
        normed_grad = normed_grad + sums_in[0, pl.ds(rows + chunk * part, part)].astype(F32)
        values = states_ref[here].astype(F32)
        inverse = lax.rsqrt(jnp.mean(values * values, axis=-1, keepdims=True) + EPS)
        scaled = normed_grad * gain
        inner = jnp.mean(scaled * values, axis=-1, keepdims=True)
        out_ref[here] = (
            inverse * scaled - values * (inverse * inverse * inverse * inner)
        ).astype(BF16)

    for way in range(2):
        pass_on(half, way, way).wait_send()

    @pl.loop(1, half)
    def _(distance):
        for way in range(2):
            for chunk in range(CHUNKS):
                pass_on(distance, way, chunk).wait_send()

    @pl.loop(0, half)
    def _(slot):
        for j in range(ny - 1):
            across(slot, j).wait_send()


def give(ny, nz, nb, grads, pos, tab, states, gain, gain_part):
    half = nz // 2
    rows, width = states.shape
    wide = ny * 2 * CAP * 8
    dma = pltpu.SemaphoreType.DMA
    return pl.pallas_call(
        functools.partial(give_kernel, ny, nz, nb),
        out_shape=(
            jax.ShapeDtypeStruct((rows, width), BF16),
            jax.ShapeDtypeStruct((1, width), F32),
        ),
        in_specs=[pl.BlockSpec(memory_space=VMEM)] * 6,
        out_specs=(pl.BlockSpec(memory_space=VMEM),) * 2,
        scratch_shapes=[
            VMEM((half, wide, width), BF16),
            VMEM((half, wide, width), BF16),
            VMEM((half, 2 * rows, width), BF16),
            VMEM((half, 2 * rows, width), BF16),
            VMEM((2 * rows, width), F32),
            VMEM((rows, width), F32),
            VMEM((nb, 8, 128), F32),
            VMEM((ny, 8, 128), F32),
            VMEM((nz, 8, 128), F32),
            dma((half, 2, CHUNKS)), dma((half, 2, CHUNKS)),
            dma((half, ny - 1)), dma((half, ny - 1)),
            dma((nb - 1,)), dma((nb - 1,)),
            dma((ny - 1,)), dma((ny - 1,)),
            dma((nz - 1,)), dma((nz - 1,)),
        ],
        compiler_params=pltpu.CompilerParams(
            collective_id=2, has_side_effects=True, vmem_limit_bytes=40 << 20
        ),
    )(grads, pos, tab, states, gain, gain_part)


def requests(owners, slots, ny, nz, held, length):
    half = nz // 2
    me = lax.axis_index("seq")
    y, z = me // nz, me % nz
    per_group = owners.shape[1]
    last = jnp.stack([owners[-1], slots[-1]])
    before = lax.ppermute(last, "seq", [(i, i + 1) for i in range(ny * nz - 1)])
    target = owners.reshape(-1)
    order = jnp.arange(target.shape[0], dtype=jnp.int32)
    earlier = (target[None, :] == target[:, None]) & (order[None, :] < order[:, None])
    rank = jnp.sum(earlier.astype(jnp.int32), axis=1)
    owner = jnp.concatenate([before[0], target])
    slot = jnp.concatenate([before[1], slots.reshape(-1)])
    rank = jnp.concatenate([jnp.full((per_group,), CAP - 1, jnp.int32), rank])
    valid = jnp.arange(owner.shape[0]) >= jnp.where(me == 0, per_group, 0)
    column, ahead = owner // nz, (owner % nz - z + nz) % nz
    way = jnp.where(ahead >= half, 1, 0)
    distance = jnp.where(ahead == 0, half, jnp.where(ahead > half, nz - ahead, ahead))
    piece = way * CAP + rank
    pieces = 2 * CAP
    place = ((distance - 1) * ny + column) * pieces + piece
    step_of = jnp.where(valid, column * half + distance - 1, -1)
    place = jnp.where(valid, place, -1)
    token = jnp.arange(length, dtype=jnp.int32)
    pos = jnp.where(place[:, None] >= 0, place[:, None] * length + token[None, :], -1).reshape(-1)
    lane = jnp.arange(ny * pieces * length, dtype=jnp.int32)
    lane_piece = jnp.where(lane // (pieces * length) == y, lane // length % pieces, -1)
    cell = jnp.arange(ny * half, dtype=jnp.int32)
    hit = (cell[:, None, None] == step_of[None, None, :]) & (
        lane_piece[None, :, None] == piece[None, None, :]
    )
    value = way * (held * length) + slot * length + 1
    found = jnp.sum(jnp.where(hit, value[None, None, :], 0), axis=-1)
    table = jnp.where(found > 0, found + lane[None, :] % length, 0).reshape(ny, half, -1)
    table = jnp.pad(table, ((0, 0), (0, max(0, 8 - half)), (0, -table.shape[2] % 128)))
    return pos, table


def on_device(ny, nz, nb, queries, out_grad, states, gain, kv_weight, owners, slots):
    held, length, enc = states.shape[1:]
    tokens, width = queries.shape[1:]
    me = lax.axis_index("seq")
    weight = lax.all_gather(kv_weight.reshape(-1, 2 * width), "batch", axis=0, tiled=True)
    pos, table = requests(owners[0], slots[0], ny, nz, held, length)
    rows = states.reshape(held * length, enc)
    gain_row = gain.reshape(1, enc)
    pages, tab = fetch(ny, nz, rows, gain_row, table, pos[:, None])
    token = jnp.arange(tokens, dtype=jnp.int32)
    group = (token + 1) // GROUP
    group = jnp.where((group == 0) & (me == 0), -1, group)[:, None]
    query_grad, grads, gain_part = attend(
        pages, group, 1.0 / gain_row, queries[0], out_grad[0], weight
    )
    state_grad, gain_grad = give(ny, nz, nb, grads, pos[None, :], tab, rows, gain_row, gain_part)
    return (
        query_grad[None],
        state_grad.reshape(1, held, length, enc),
        gain_grad.reshape(enc),
    )


def solution(mesh):
    ny = Y_SIZE
    nz = mesh.shape["seq"] // ny
    nb = mesh.shape["batch"]
    return jax.shard_map(
        functools.partial(on_device, ny, nz, nb),
        mesh=mesh,
        in_specs=(
            P("batch", "seq", None),
            P("batch", "seq", None),
            P("batch", "seq", None, None),
            P(),
            P("batch", None, None),
            P("batch", "seq", None),
            P("batch", "seq", None),
        ),
        out_specs=(P("batch", "seq", None), P("batch", "seq", None, None), P()),
        check_vma=False,
    )
```

time: 443 us -> 165 us (0.37)
  waiting for transfers between devices: 161 us -> 0.04 us
  Pallas kernels: 0 us -> 134 us
  blocking collectives: 99.7 us -> 0 us
  local copies, waits for them, and re-layouts: 64.6 us -> 10.3 us
  matrix products: 39.6 us -> 0 us
  starting transfers between devices: 38.5 us -> 3.86 us
  other arithmetic: 22 us -> 2.15 us
    all_to_all x3 -> x0, waiting for transfers between devices: 161 us -> none  [the longest x1 85.9 us: on_device(): lax.all_to_all(replies.reshape(peer_count, capacity, length * enc_width),...]
    pallas_call x0 -> x3, Pallas kernels: none -> 134 us  [the longest x1 60.4 us: fetch(): pl.pallas_call(functools.partial(fetch_kernel, ny, nz), out_shape=(jax.Sh...]
    psum x1 -> x0, blocking collectives: 99.7 us -> none  [on_device(): lax.psum(jnp.sum(normed_grad * values * inverse, axis=(0, 1)), ('seq', 'b...]
    dot_general x14 -> x0, matrix products: 39.6 us -> none  [the longest x1 19.9 us: block_backward(): jnp.einsum('uhqk,ukhe->uqhe', grad_scores, key_block, preferred_element_t...]
    all_to_all x3 -> x0, starting transfers between devices: 33.8 us -> none  [the longest x1 18.7 us: on_device(): lax.all_to_all(wanted.reshape(peer_count, capacity), 'seq', split_axis=0,...]
    reshape x10 -> x1, local copies, waits for them, and re-layouts: 26 us -> 0.69 us  [on_device(): gain_row = gain.reshape(1, enc)]
    all_gather x1 -> x0, local copies, waits for them, and re-layouts: 18.8 us -> none  [on_device(): gathered = lax.all_gather(kv_weight, 'batch', axis=0, tiled=True)]
    sub x2 -> x0, other arithmetic: 16.9 us -> none  [the longest x1 16.9 us: block_backward(): grad_probability - delta_sum]
  transfers between devices with their start and end apart: 6 -> 2, of which waited for: 3 -> 0; matrix products, arithmetic and copies ran while one was open for 18% -> 3% of each run, Pallas kernels for 0% -> 37%
where the time goes in v1:
time: 165 us; the launch traced here: 164 us
  Pallas kernels  134 us (81%)
  between operations  14.2 us (9%)
  local copies, waits for them, and re-layouts  10.3 us (6%)
  starting transfers between devices  3.86 us (2%)
  other arithmetic  2.15 us (1%)
    pallas_call x1, Pallas kernels, fetch(): pl.pallas_call(functools.partial(fetch_kernel, ny, nz), out_shape=(jax.Sh...  60.4 us
    pallas_call x1, Pallas kernels, give(): pl.pallas_call(functools.partial(give_kernel, ny, nz, nb), out_shape=(jax...  58 us
    pallas_call x1, Pallas kernels, attend(): pl.pallas_call(attend_kernel, grid=(steps,), out_shape=(jax.ShapeDtypeStr...  15.2 us
    unnamed x12, local copies, waits for them, and re-layouts  7.2 us
    ppermute x1, starting transfers between devices, requests(): before = lax.ppermute(last, 'seq', [(i, i + 1) for i in range(ny * nz - 1)])  3.82 us
  transfers between devices with their start and end apart: 2, of which 0 were waited for; matrix products, arithmetic and copies ran while one was open for 3% of the time, Pallas kernels for 37%

profile of v1, /device:TPU:6, one launch (start us, length us, event | category | flops | bytes accessed | tf_op | source)
XLA Modules:
  0.0 164.2 jit_solution(17413455164417091198)
XLA Ops:
  7.2 0.0 copy-start.2
  7.2 0.0 copy-start.1
  7.2 0.0 all-gather.2.cloned.1.call-start
  7.2 2.5 %copy.12 = bf16[14,8,2,2048]{3,1,2,0:T(8,128)(2,1)} copy(bf16[14,8,2,2048]{3,2,1,0:T(2,128)(2,1)} %bitcast.28) | data formatting | bytes 1835008
  9.7 0.0 all-gather.2.cloned.1.call-update
  9.7 0.7 slice_bitcast_fusion.2
  10.5 3.8 %collective-permute-start = (s32[2,8]{1,0:T(2,128)S(1)}, s32[2,8]{1,0:T(2,128)S(1)}, u32[]{:S(2)}, u32[]{:S(2)}) collective-permute-start(s32[2,8]{1,0:T(2,128)S(1)} %pad_add_fusion), channel_id=1, source_target_pairs={{0,8},{8,16},{16,24},{24,32},{32,40},{40,48},{48,56},{56,64},{64,7... | collective-permute-start | bytes 200 | tf_op jit(solution)/shard_map/ppermute | solution.py:517
  14.3 0.8 concatenate.51
  15.1 0.8 concatenate.55
  15.8 0.7 reshape.460.gain_ref
  16.5 0.7 broadcast_divide_fusion
  17.2 0.2 convert_reduce_fusion
  17.4 0.0 collective-permute-done
  17.5 0.1 broadcast_compare_fusion.1
  17.6 0.1 add_select_fusion.1
  17.7 0.1 select_n.207.pos_ref
  17.7 0.1 select_n.208.pos_ref
  17.8 0.1 compare_select_fusion.10
  17.9 0.1 broadcast_compare_fusion
  18.0 0.3 select_reduce_fusion
  18.3 0.0 copy-start.3
  18.3 0.9 copy-done.3
  19.3 60.4 %shard_map.94 = (bf16[192,896]{1,0:T(8,128)(2,1)S(1)}, s32[8,256]{1,0:T(8,128)S(1)}) custom-call(bf16[128,896]{1,0:T(8,128)(2,1)S(1)} %bitcast.24, f32[1,896]{1,0:T(1,128)S(1)} %reshape.460.gain_ref, s32[4,8,256]{2,1,0:T(8,128)S(1)} %pad.5.table_ref, s32[192,1]{1,0:T(8,128)S(1)} %select_n.208.pos_ref), custom_call_target="tpu_custom_call" | custom-call | flops 2000000000 | bytes 100000000 | tf_op jit(solution)/shard_map/pallas_call | solution.py:197
  79.7 0.0 all-gather.2.cloned.1.call-done.wk_ref.wv_ref
  79.7 0.0 copy-done.2
  79.7 0.0 copy-done.1
  79.7 0.0 copy-start
  79.7 3.1 %copy-done = bf16[896,4096]{1,0:T(8,128)(2,1)S(1)} copy-done((bf16[896,4096]{1,0:T(8,128)(2,1)S(1)}, bf16[896,4096]{1,0:T(8,128)(2,1)}, u32[]{:S(2)}) %copy-start) | copy-done | bytes 7340056
  82.8 0.0 copy-start.4
  82.8 15.2 %shard_map.95 = (bf16[128,2048]{1,0:T(8,128)(2,1)}, bf16[192,896]{1,0:T(8,128)(2,1)S(1)}, f32[1,896]{1,0:T(1,128)S(1)}) custom-call(bf16[192,896]{1,0:T(8,128)(2,1)S(1)} %get-tuple-element.10.pages_ref, s32[128,1]{1,0:T(8,128)S(1)} %and_select_fusion.group_ref, f32[1,896]{1,0:T(1,128)S(1)} %div.78.rgain_ref, bf16[128,2048]{1,0:T(8,128)(2,1)S(1)} %bitcast.22, ...), custom_call_target="tpu_custom_call" | custom-call | tf_op jit(solution)/shard_map/pallas_call | solution.py:281
  98.0 0.0 copy-done.4
  98.0 58.0 %shard_map.96 = (bf16[128,896]{1,0:T(8,128)(2,1)S(1)}, f32[1,896]{1,0:T(1,128)S(1)}) custom-call(bf16[192,896]{1,0:T(8,128)(2,1)S(1)} %get-tuple-element.12.grad_ref, s32[1,192]{1,0:T(1,128)S(1)} %select_n.207.pos_ref, s32[8,256]{1,0:T(8,128)S(1)} %get-tuple-element.13.tab_ref, bf16[128,896]{1,0:T(8,128)(2,1)S(1)} %bitcast.25, ...), custom_call_target="tpu_custom_call" | custom-call | tf_op jit(solution)/shard_map/pallas_call | solution.py:481
  156.0 0.6 reduce
  156.6 0.7 copy.14
  (10 shorter events, 0.1 us)
Async XLA Ops:
  7.2 72.5 %copy-start.2 = (bf16[1,128,2048]{2,1,0:T(8,128)(2,1)S(1)}, bf16[1,128,2048]{2,1,0:T(8,128)(2,1)}, u32[]{:S(2)}) copy-start(bf16[1,128,2048]{2,1,0:T(8,128)(2,1)} %param.8) | copy-start | bytes 1572868
  7.2 72.5 %copy-start.1 = (bf16[1,128,2048]{2,1,0:T(8,128)(2,1)S(1)}, bf16[1,128,2048]{2,1,0:T(8,128)(2,1)}, u32[]{:S(2)}) copy-start(bf16[1,128,2048]{2,1,0:T(8,128)(2,1)} %param.7) | copy-start | bytes 1572868
  7.2 72.5 %all-gather.2.cloned.1.call-start = ((), (), s32[]{:S(2)}) async-start(), calls=%async_computation | async-start | bytes 8257536 | tf_op jit(solution)/shard_map/all_gather | solution.py:553
  10.5 7.0 %collective-permute-start = (s32[2,8]{1,0:T(2,128)S(1)}, s32[2,8]{1,0:T(2,128)S(1)}, u32[]{:S(2)}, u32[]{:S(2)}) collective-permute-start(s32[2,8]{1,0:T(2,128)S(1)} %pad_add_fusion), channel_id=1, source_target_pairs={{0,8},{8,16},{16,24},{24,32},{32,40},{40,48},{48,56},{56,64},{64,7... | collective-permute-start | bytes 200 | tf_op jit(solution)/shard_map/ppermute | solution.py:517
  18.3 0.9 copy-start.3
  79.7 3.1 %copy-start = (bf16[896,4096]{1,0:T(8,128)(2,1)S(1)}, bf16[896,4096]{1,0:T(8,128)(2,1)}, u32[]{:S(2)}) copy-start(bf16[896,4096]{1,0:T(8,128)(2,1)} %all-gather.2.cloned.1.call-done.wk_ref.wv_ref) | copy-start | bytes 22020100
  82.8 15.2 %copy-start.4 = (bf16[1,16,8,896]{3,2,1,0:T(8,128)(2,1)S(1)}, bf16[1,16,8,896]{3,2,1,0:T(8,128)(2,1)}, u32[]{:S(2)}) copy-start(bf16[1,16,8,896]{3,2,1,0:T(8,128)(2,1)} %param.9) | copy-start | bytes 688132
Sparse Core Ops, SparseCore 0:
  10.1 55.5 all-gather.1

commit v2 on v0

v2 whole, which is shorter than its diff:
```python
import functools
import math

import jax
import jax.numpy as jnp
from jax import lax
from jax.experimental import pallas as pl
from jax.experimental.pallas import tpu as pltpu
from jax.sharding import PartitionSpec as P

HEAD_DIM = 128
GROUP = 64
EPS = 1e-06
Y_SIZE = 4
CHUNKS = 2
X_CORES = 2
CAP = 3

MESH = pl.DeviceIdType.MESH
VMEM = pltpu.VMEM
F32 = jnp.float32
BF16 = jnp.bfloat16


def one_hot(mask):
    return jnp.where(mask, 1.0, 0.0).astype(BF16)


class Place:
    def __init__(self, ny, nz):
        me = lax.axis_index("seq")
        self.ny, self.nz = ny, nz
        self.y = lax.div(me, nz)
        self.z = lax.rem(me, nz)
        self.up = self.at(self.y, lax.rem(self.z + 1, nz))
        self.down = self.at(self.y, lax.rem(self.z + nz - 1, nz))
        self.across = [lax.rem(self.y + j, ny) for j in range(1, ny)]

    def at(self, y, z):
        return {"seq": y * self.nz + z}


def remote(src, dst, send_sem, recv_sem, device):
    return pltpu.make_async_remote_copy(
        src_ref=src,
        dst_ref=dst,
        send_sem=send_sem,
        recv_sem=recv_sem,
        device_id=device,
        device_id_type=MESH,
    )

MINOR = (((1,), (1,)), ((), ()))
MAJOR = (((0,), (0,)), ((), ()))


def iota(shape, dim):
    return lax.broadcasted_iota(jnp.int32, shape, dim)


def inverse_norm(values):
    return lax.rsqrt(jnp.mean(values * values, axis=-1, keepdims=True) + EPS)


def kernel(
    ny, nz, nb,
    q_ref, do_ref, states_ref, gain_ref, kv_ref, ids_ref,
    dq_ref, out_ref, gain_out_ref,
    ring, tabs, tab, pos, outs, recv, acc, mine, grad_rows, ids, ids_before, weight,
    back, sums_in, sums_out, added, own, by_batch, by_y, by_z,
    ring_send, ring_recv, y_send, y_recv, tab_send, tab_recv, id_send, id_recv, w_send, w_recv,
    sum_send, sum_recv, back_send, back_recv, b_send, b_recv, gy_send, gy_recv, z_send, z_recv,
):
    half = nz // 2
    place = Place(ny, nz)
    y, z, b = place.y, place.z, lax.axis_index("batch")
    me = y * nz + z
    rows, width = states_ref.shape
    part = rows // CHUNKS
    wide = outs.shape[1]
    block = wide // ny
    wanted = acc.shape[0]
    steps_pad = tab.shape[0]
    count = ny * nz
    following = {"seq": lax.rem(me + 1, count)}
    preceding = {"seq": lax.rem(me + count - 1, count)}
    b_peers = [lax.rem(b + j, nb) for j in range(1, nb)]
    z_peers = [lax.rem(z + j, nz) for j in range(1, nz)]
    core = lax.rem(b, X_CORES)
    right = lax.rem(b + X_CORES, nb)
    left = lax.rem(b + nb - X_CORES, nb)
    opposite = lax.rem(b + 2 * X_CORES, nb)
    sibling = b + 1 - 2 * core


    def ring_part(slot, way, chunk):
        return ring.at[slot, pl.ds(way * rows + chunk * part, part)]

    def forward(slot, way, chunk):
        far = isinstance(slot, int) and slot == half - 1
        first = isinstance(slot, int) and slot == 0
        src = ring_part(half - 1, 0, chunk) if first else ring_part(slot - 1, way, chunk)
        dst = ring_part(slot, 1, chunk) if far else ring_part(slot, way, chunk)
        return remote(
            src,
            dst,
            ring_send.at[slot, way, chunk],
            ring_recv.at[slot, way, chunk],
            place.down if way == 0 else place.up,
        )

    def exchange(into, send, arrived, slot, j):
        there = place.across[j]
        return remote(
            outs.at[slot, pl.ds(there * block, block)],
            into.at[slot, pl.ds(y * block, block)],
            send.at[slot, j],
            arrived.at[slot, j],
            place.at(there, z),
        )

    def across(slot, j):
        return exchange(recv, y_send, y_recv, slot, j)

    def return_across(slot, j):
        return exchange(back, back_send, back_recv, slot, j)

    def table_copy(j):
        there = place.across[j]
        return remote(
            tabs.at[ny + there], tabs.at[y], tab_send.at[j], tab_recv.at[j], place.at(there, z)
        )


    depth = kv_ref.shape[0]
    cut = (depth + 31) // 32 * 16
    weight_parts = ((0, cut), (cut, depth - cut))

    def weight_copy(channel, number):
        first, size = weight_parts[number]
        if channel == 2:
            shard, device = (left, right) if number == 0 else (right, left)
        else:
            shard = (b, b, None, b, left, right, opposite)[channel]
            device = (right, left, None, sibling, sibling, sibling, sibling)[channel]
        there = weight.at[pl.ds(pl.multiple_of(shard * depth + first, 16), size)]
        return remote(
            kv_ref.at[pl.ds(first, size)] if channel in (0, 1, 3) else there,
            there,
            w_send.at[channel, number],
            w_recv.at[channel, number],
            {"batch": device},
        )

    def weights_one():
        weight_copy(0, 0).wait_recv()
        weight_copy(2, 0).start()
        weight_copy(4, 0).start()
        weight_copy(1, 1).wait_recv()
        weight_copy(2, 1).start()
        weight_copy(5, 1).start()

    def weights_two():
        weight_copy(0, 1).wait_recv()
        weight_copy(4, 1).start()
        weight_copy(1, 0).wait_recv()
        weight_copy(5, 0).start()

    def weights_three():
        for number in range(2):
            weight_copy(2, number).wait_recv()
            weight_copy(6, number).start()


    def part_of(ref, slot, way, chunk):
        return ref.at[slot, pl.ds(way * rows + chunk * part, part)]

    def pass_on(distance, way, chunk):
        far = isinstance(distance, int) and distance == half
        return remote(
            part_of(sums_out, distance - 1, 1 if far else way, chunk),
            part_of(sums_in, distance - 1, way, chunk),
            sum_send.at[distance - 1, way, chunk],
            sum_recv.at[distance - 1, way, chunk],
            place.up if way == 0 else place.down,
        )


    def b_copy(j):
        return remote(
            by_batch.at[b], by_batch.at[b], b_send.at[j], b_recv.at[j], {"batch": b_peers[j]}
        )

    def gy_copy(j):
        return remote(
            by_y.at[y], by_y.at[y], gy_send.at[j], gy_recv.at[j], place.at(place.across[j], z)
        )

    def z_copy(j):
        return remote(
            by_z.at[z], by_z.at[z], z_send.at[j], z_recv.at[j], place.at(y, z_peers[j])
        )

    def total(ref):
        result = ref[0]
        for i in range(1, ref.shape[0]):
            result = result + ref[i]
        return result


    values = states_ref[...].astype(F32)
    ring[half - 1, :rows] = (values * inverse_norm(values) * gain_ref[...]).astype(BF16)
    ids[...] = jnp.zeros_like(ids)
    ids[: ids_ref.shape[0], : ids_ref.shape[1]] = ids_ref[...]

    barrier = pltpu.get_barrier_semaphore()
    peers = (
        [{"batch": peer} for peer in b_peers]
        + [place.at(there, z) for there in place.across]
        + [place.at(y, there) for there in z_peers]
        + [preceding]
    )
    for peer in peers:
        pl.semaphore_signal(barrier, inc=1, device_id=peer, device_id_type=MESH)
    pl.semaphore_wait(barrier, len(peers))

    ids_copy = remote(ids, ids_before, id_send, id_recv, following)
    ids_copy.start()
    for chunk in range(CHUNKS):
        for way in range(2):
            forward(0, way, chunk).start()
    for number in range(2):
        weight_copy(0, number).start()
        weight_copy(1, 1 - number).start()
    for number in range(2):
        weight_copy(3, number).start()
    acc[...] = jnp.zeros_like(acc)
    weight[pl.ds(pl.multiple_of(b * depth, 16), depth)] = kv_ref[...]


    pieces = 2 * CAP
    length = block // pieces
    own_count = ids_ref.shape[1]
    group = own_count // 2
    request_count = own_count + group
    ids_copy.wait()
    lane = iota(ids.shape, 1)
    merged = jnp.where(lane < own_count, ids[...], pltpu.roll(ids_before[...], group, 1))
    known = (lane < own_count) | ((lane < request_count) & (me > 0))
    owner = jnp.where(known, merged, -1)[0:1]
    slot_id = merged[1:2]
    lane = lane[0:1]
    rank = jnp.where(lane < own_count, 0, CAP - 1)
    wide_owner = jnp.broadcast_to(owner, ids.shape)
    for shift in range(1, 2 * group):
        other = pltpu.roll(wide_owner, shift, 1)[0:1]
        source = lane - shift
        same = (other == owner) & (source >= 0) & (source < group)
        rank = jnp.where(same & (lane >= group) & (lane < own_count), 1, rank)
    column = jnp.zeros_like(owner)
    for j in range(1, ny):
        column = column + jnp.where(owner >= j * nz, 1, 0)
    ahead = owner - column * nz - z
    ahead = jnp.where(ahead < 0, ahead + nz, ahead)
    way = jnp.where(ahead >= half, 1, 0)
    distance = jnp.where(ahead == 0, half, jnp.where(ahead > half, nz - ahead, ahead))
    piece = way * CAP + rank
    cell = jnp.where(owner >= 0, column * steps_pad + distance - 1, -1)
    number = jnp.where(owner >= 0, ((distance - 1) * ny + column) * pieces + piece, -1)
    value = way * rows + slot_id * length + 1

    table_rows, table_lanes = ny * steps_pad, tab.shape[1]
    lanes_of = (table_lanes, lane.shape[1])
    row = iota(lanes_of, 0) - y * block
    row_piece = jnp.where((row >= 0) & (row < block), lax.div(row, length), -1)
    chosen = jnp.where(row_piece == piece, value, 0).astype(F32).astype(BF16)
    cells = one_hot(iota((table_rows, lane.shape[1]), 0) == cell)
    found = lax.dot_general(cells, chosen, MINOR, preferred_element_type=F32).astype(jnp.int32)
    token = lax.rem(iota((table_rows, table_lanes), 1), length)
    table = jnp.where(found > 0, found + token, 0)
    for j in range(ny):
        tabs[ny + j] = table[j * steps_pad : (j + 1) * steps_pad]
    for j in range(ny - 1):
        table_copy(j).start()
    tabs[pl.ds(y, 1)] = tabs[pl.ds(ny + y, 1)]

    spread_of = (pos.shape[1], lane.shape[1])
    spread = one_hot(lax.div(iota(spread_of, 0), length) == iota(spread_of, 1))
    numbers = jnp.broadcast_to(number, ids.shape).astype(F32).astype(BF16)
    placed = lax.dot_general(numbers, spread, MINOR, preferred_element_type=F32).astype(jnp.int32)
    token = lax.rem(iota(placed.shape, 1), length)
    pos[...] = jnp.where(placed >= 0, placed * length + token, -1)

    for j in range(ny - 1):
        table_copy(j).wait()
    asked = tabs[0]
    for j in range(1, ny):
        asked = asked + tabs[j]
    tab[...] = asked


    def selected(slot):
        row = tab[pl.ds(slot, 1), :wide]
        return one_hot(iota((2 * rows, wide), 0) + 1 == row)

    def placing(slot):
        return one_hot(iota((wide, wanted), 0) + slot * wide == pos[0:1, :wanted])

    def pick(slot):
        outs[slot] = lax.dot_general(
            selected(slot), ring[slot], MAJOR, preferred_element_type=F32
        ).astype(BF16)
        for j in range(ny - 1):
            across(slot, j).start()
        recv[slot, pl.ds(y * block, block)] = outs[slot, pl.ds(y * block, block)]

    def take(slot):
        for j in range(ny - 1):
            across(slot, j).wait_recv()
        acc[...] += lax.dot_general(placing(slot), recv[slot], MAJOR, preferred_element_type=F32)

    def near(slot, last):
        for chunk in range(CHUNKS):
            for way in range(2):
                forward(slot, way, chunk).wait_recv()
                if not last:
                    forward(slot + 1, way, chunk).start()
                elif way == chunk:
                    forward(half - 1, way, chunk).start()
        pick(slot)

    services = {2: weights_one, 4: weights_two}
    near(0, half == 2)
    if half > 2:

        @pl.loop(1, half - 2)
        def _(slot):
            near(slot, False)
            take(slot - 1)
            for at, service in services.items():
                if at < half - 2:
                    pl.when(slot == at)(service)

        near(half - 2, True)
        take(half - 3)
    for at, service in services.items():
        if at >= half - 2:
            service()
    weights_three()
    for way in range(2):
        forward(half - 1, way, way).wait_recv()
    pick(half - 1)
    take(half - 2)
    for channel in range(3, 7):
        for number in range(2):
            weight_copy(channel, number).wait_recv()
    take(half - 1)
    mine[...] = acc[...].astype(BF16)

    for way in range(2):
        forward(half - 1, way, way).wait_send()

    @pl.loop(0, half - 1)
    def _(slot):
        for way in range(2):
            for chunk in range(CHUNKS):
                remote(
                    ring_part(0, way, chunk),
                    ring_part(0, way, chunk),
                    ring_send.at[slot, way, chunk],
                    ring_recv.at[slot, way, chunk],
                    place.down if way == 0 else place.up,
                ).wait_send()

    @pl.loop(0, half)
    def _(slot):
        for j in range(ny - 1):
            across(slot, j).wait_send()

    for channel in range(7):
        for number in range(2):
            weight_copy(channel, number).wait_send()


    tokens = q_ref.shape[0]
    scaling = 1.0 / math.sqrt(HEAD_DIM)
    turn = lax.div(iota((tokens, wanted), 0) + 1, GROUP)
    key_group = lax.div(iota((tokens, wanted), 1), GROUP)
    mask = lax.rem(turn + 2, 3) == key_group
    mask = mask & ((turn > 0) | (me > 0))
    pages = mine[...]
    heads_wide = 2 * HEAD_DIM
    steps = q_ref.shape[1] // heads_wide
    acc[...] = jnp.zeros_like(acc)

    @pl.loop(0, steps)
    def _(step):
        here = pl.ds(pl.multiple_of(step * heads_wide, heads_wide), heads_wide)
        there = pl.ds(
            pl.multiple_of((steps + step) * heads_wide, heads_wide), heads_wide
        )
        key_weight, value_weight = weight[:, here], weight[:, there]
        key_all = jnp.dot(pages, key_weight, preferred_element_type=F32).astype(BF16)
        value_all = jnp.dot(pages, value_weight, preferred_element_type=F32).astype(BF16)
        queries, grads = q_ref[:, here], do_ref[:, here]
        query_grads, key_grads, value_grads = [], [], []
        for head in range(heads_wide // HEAD_DIM):
            columns = slice(head * HEAD_DIM, (head + 1) * HEAD_DIM)
            query, grad = queries[:, columns], grads[:, columns]
            key, val = key_all[:, columns], value_all[:, columns]
            scores = lax.dot_general(query, key, MINOR, preferred_element_type=F32) * scaling
            weights = jnp.where(mask, jnp.exp(jnp.where(mask, scores, 0.0)), 0.0)
            over = jnp.sum(weights, axis=-1, keepdims=True)
            probability = weights / jnp.where(over == 0.0, 1.0, over)
            grad_probability = lax.dot_general(grad, val, MINOR, preferred_element_type=F32)
            delta = jnp.sum(probability * grad_probability, axis=-1, keepdims=True)
            grad_scores = (probability * (grad_probability - delta) * scaling).astype(BF16)
            low = probability.astype(BF16)
            query_grads.append(jnp.dot(grad_scores, key, preferred_element_type=F32))
            key_grads.append(lax.dot_general(grad_scores, query, MAJOR, preferred_element_type=F32))
            value_grads.append(lax.dot_general(low, grad, MAJOR, preferred_element_type=F32))
        dq_ref[:, here] = jnp.concatenate(query_grads, axis=1).astype(BF16)
        key_grad = jnp.concatenate(key_grads, axis=1).astype(BF16)
        value_grad = jnp.concatenate(value_grads, axis=1).astype(BF16)
        change = lax.dot_general(key_grad, key_weight, MINOR, preferred_element_type=F32)
        change += lax.dot_general(value_grad, value_weight, MINOR, preferred_element_type=F32)
        acc[...] += change

    grad_rows[...] = acc[...].astype(BF16)


    def scatter(slot):
        outs[slot] = jnp.dot(placing(slot), grad_rows[...], preferred_element_type=F32).astype(BF16)
        for j in range(ny - 1):
            return_across(slot, j).start()
        back[slot, pl.ds(y * block, block)] = outs[slot, pl.ds(y * block, block)]

    def gather(slot):
        for j in range(ny - 1):
            return_across(slot, j).wait_recv()
        added[...] = jnp.dot(selected(slot), back[slot], preferred_element_type=F32)

    def relay(distance, first):
        gather(distance - 1)
        for chunk in range(CHUNKS):
            for way in range(2):
                here = pl.ds(way * rows + chunk * part, part)
                total_here = added[here]
                if not first or way == chunk:
                    pass_on(distance + 1, way, chunk).wait_recv()
                    total_here = total_here + sums_in[distance, here].astype(F32)
                sums_out[distance - 1, here] = total_here.astype(BF16)
                pass_on(distance, way, chunk).start()

    def gain_one():
        lanes = width // 128
        products = jnp.sum(grad_rows[...].astype(F32) * mine[...].astype(F32), axis=0, keepdims=True)
        products = products / gain_ref[...]
        by_batch[pl.ds(b, 1)] = jnp.zeros_like(by_batch[pl.ds(b, 1)])
        for i in range(lanes):
            by_batch[b, i : i + 1] = products[:, i * 128 : (i + 1) * 128]
        for j in range(nb - 1):
            b_copy(j).start()

    def gain_two():
        for j in range(nb - 1):
            b_copy(j).wait()
        by_y[y] = total(by_batch)
        for j in range(ny - 1):
            gy_copy(j).start()

    def gain_three():
        for j in range(ny - 1):
            gy_copy(j).wait()
        by_z[z] = total(by_y)
        for j in range(nz - 1):
            z_copy(j).start()

    scatter(half - 1)
    scatter(half - 2)
    gather(half - 1)
    own[...] = added[:rows]
    sums_out[half - 1, pl.ds(rows, rows)] = added[pl.ds(rows, rows)].astype(BF16)
    for way in range(2):
        pass_on(half, way, way).start()
    gain_one()
    if half > 2:
        scatter(half - 3)
    relay(half - 1, True)
    gain_two()
    if half > 2:

        @pl.loop(0, half - 3)
        def _(i):
            distance = half - 2 - i
            scatter(distance - 2)
            relay(distance, False)

    gain_three()
    if half > 2:
        relay(1, False)

    for j in range(nz - 1):
        z_copy(j).wait()
    result = total(by_z)
    for i in range(width // 128):
        gain_out_ref[:, i * 128 : (i + 1) * 128] = result[i : i + 1]

    for chunk in range(CHUNKS):
        here = pl.ds(chunk * part, part)
        for way in range(2):
            pass_on(1, way, chunk).wait_recv()
        normed_grad = own[here] + sums_in[0, here].astype(F32)
        normed_grad = normed_grad + sums_in[0, pl.ds(rows + chunk * part, part)].astype(F32)
        values = states_ref[here].astype(F32)
        inverse = inverse_norm(values)
        scaled = normed_grad * gain_ref[...]
        inner = jnp.mean(scaled * values, axis=-1, keepdims=True)
        out_ref[here] = (
            inverse * scaled - values * (inverse * inverse * inverse * inner)
        ).astype(BF16)

    for way in range(2):
        pass_on(half, way, way).wait_send()

    @pl.loop(1, half)
    def _(distance):
        for way in range(2):
            for chunk in range(CHUNKS):
                pass_on(distance, way, chunk).wait_send()

    @pl.loop(0, half)
    def _(slot):
        for j in range(ny - 1):
            return_across(slot, j).wait_send()


def on_device(ny, nz, nb, queries, out_grad, states, gain, kv_weight, owners, slots):
    held, length, enc = states.shape[1:]
    tokens, width = queries.shape[1:]
    half, rows = nz // 2, held * length
    wanted = owners.shape[1] * owners.shape[2] * 3 // 2 * length
    wide = ny * 2 * CAP * length
    table = (max(8, half), wide + -wide % 128)
    ids = jnp.stack([owners.reshape(-1), slots.reshape(-1)])
    dma = pltpu.SemaphoreType.DMA
    query_grad, state_grad, gain_grad = pl.pallas_call(
        functools.partial(kernel, ny, nz, nb),
        out_shape=(
            jax.ShapeDtypeStruct((tokens, width), BF16),
            jax.ShapeDtypeStruct((rows, enc), BF16),
            jax.ShapeDtypeStruct((1, enc), F32),
        ),
        in_specs=[pl.BlockSpec(memory_space=VMEM)] * 6,
        out_specs=(pl.BlockSpec(memory_space=VMEM),) * 3,
        scratch_shapes=[
            VMEM((half, 2 * rows, enc), BF16),
            VMEM((2 * ny,) + table, jnp.int32),
            VMEM(table, jnp.int32),
            VMEM((8, wanted + -wanted % 128), jnp.int32),
            VMEM((half, wide, enc), BF16),
            VMEM((half, wide, enc), BF16),
            VMEM((wanted, enc), F32),
            VMEM((wanted, enc), BF16),
            VMEM((wanted, enc), BF16),
            VMEM((8, 128), jnp.int32),
            VMEM((8, 128), jnp.int32),
            VMEM((enc, 2 * width), BF16),
            VMEM((half, wide, enc), BF16),
            VMEM((half, 2 * rows, enc), BF16),
            VMEM((half, 2 * rows, enc), BF16),
            VMEM((2 * rows, enc), F32),
            VMEM((rows, enc), F32),
            VMEM((nb, 8, 128), F32),
            VMEM((ny, 8, 128), F32),
            VMEM((nz, 8, 128), F32),
            dma((half, 2, CHUNKS)), dma((half, 2, CHUNKS)),
            dma((half, ny - 1)), dma((half, ny - 1)),
            dma((ny - 1,)), dma((ny - 1,)),
            dma, dma,
            dma((7, 2)), dma((7, 2)),
            dma((half, 2, CHUNKS)), dma((half, 2, CHUNKS)),
            dma((half, ny - 1)), dma((half, ny - 1)),
            dma((nb - 1,)), dma((nb - 1,)),
            dma((ny - 1,)), dma((ny - 1,)),
            dma((nz - 1,)), dma((nz - 1,)),
        ],
        compiler_params=pltpu.CompilerParams(
            collective_id=1, has_side_effects=True, vmem_limit_bytes=48 << 20
        ),
    )(
        queries[0], out_grad[0], states.reshape(rows, enc), gain.reshape(1, enc),
        kv_weight.reshape(-1, 2 * width), ids,
    )
    return (
        query_grad[None],
        state_grad.reshape(1, held, length, enc),
        gain_grad.reshape(enc),
    )


def solution(mesh):
    ny = Y_SIZE
    nz = mesh.shape["seq"] // ny
    nb = mesh.shape["batch"]
    return jax.shard_map(
        functools.partial(on_device, ny, nz, nb),
        mesh=mesh,
        in_specs=(
            P("batch", "seq", None),
            P("batch", "seq", None),
            P("batch", "seq", None, None),
            P(),
            P("batch", None, None),
            P("batch", "seq", None),
            P("batch", "seq", None),
        ),
        out_specs=(P("batch", "seq", None), P("batch", "seq", None, None), P()),
        check_vma=False,
    )
```

time: 443 us -> 136 us (0.31)
  waiting for transfers between devices: 161 us -> 0 us
  Pallas kernels: 0 us -> 130 us
  blocking collectives: 99.7 us -> 0 us
  local copies, waits for them, and re-layouts: 64.6 us -> 3.91 us
  matrix products: 39.6 us -> 0 us
  starting transfers between devices: 38.5 us -> 0 us
  other arithmetic: 22 us -> 0.62 us
  between operations: 14.5 us -> 0.73 us
    all_to_all x3 -> x0, waiting for transfers between devices: 161 us -> none  [the longest x1 85.9 us: on_device(): lax.all_to_all(replies.reshape(peer_count, capacity, length * enc_width),...]
    pallas_call x0 -> x1, Pallas kernels: none -> 130 us  [on_device(): pl.pallas_call(functools.partial(kernel, ny, nz, nb), out_shape=(jax.Shap...]
    psum x1 -> x0, blocking collectives: 99.7 us -> none  [on_device(): lax.psum(jnp.sum(normed_grad * values * inverse, axis=(0, 1)), ('seq', 'b...]
    dot_general x14 -> x0, matrix products: 39.6 us -> none  [the longest x1 19.9 us: block_backward(): jnp.einsum('uhqk,ukhe->uqhe', grad_scores, key_block, preferred_element_t...]
    all_to_all x3 -> x0, starting transfers between devices: 33.8 us -> none  [the longest x1 18.7 us: on_device(): lax.all_to_all(wanted.reshape(peer_count, capacity), 'seq', split_axis=0,...]
    reshape x10 -> x1, local copies, waits for them, and re-layouts: 26 us -> 0.01 us  [on_device(): gain.reshape(1, enc)]
    all_gather x1 -> x0, local copies, waits for them, and re-layouts: 18.8 us -> none  [on_device(): gathered = lax.all_gather(kv_weight, 'batch', axis=0, tiled=True)]
    sub x2 -> x0, other arithmetic: 16.9 us -> none  [the longest x1 16.9 us: block_backward(): grad_probability - delta_sum]
  transfers between devices with their start and end apart: 6 -> 0, of which waited for: 3 -> 0; matrix products, arithmetic and copies ran while one was open for 18% -> 0% of each run, Pallas kernels for 0% -> 0%
where the time goes in v2:
time: 136 us; the launch traced here: 135 us
  Pallas kernels  130 us (96%)
  local copies, waits for them, and re-layouts  3.91 us (3%)
    pallas_call x1, Pallas kernels, on_device(): pl.pallas_call(functools.partial(kernel, ny, nz, nb), out_shape=(jax.Shap...  130 us
    unnamed x15, local copies, waits for them, and re-layouts  3.74 us

profile of v2, /device:TPU:6, one launch (start us, length us, event | category | flops | bytes accessed | tf_op | source)
XLA Modules:
  0.0 134.9 jit_solution(13426145012193404479)
XLA Ops:
  0.6 0.0 copy-start.4
  0.6 0.0 copy-start.5
  0.7 0.0 copy-start.3
  0.7 0.7 copy-done.4
  1.3 0.1 stack_reshape.6
  1.4 0.0 copy-done.5
  1.4 0.1 stack_reshape.7
  1.5 0.0 copy-done.3
  1.5 0.0 copy-start
  1.5 0.0 copy-start.1
  1.5 0.0 copy-start.2
  1.5 1.6 %copy.10 = bf16[14,8,2,2048]{3,1,2,0:T(8,128)(2,1)S(1)} copy(bf16[14,8,2,2048]{3,2,1,0:T(2,128)(2,1)} %bitcast.13) | data formatting | bytes 1835008
  3.1 0.0 copy-done
  3.1 0.0 copy-done.1
  3.1 0.0 copy-done.2
  3.2 129.7 %shard_map.94 = (bf16[128,2048]{1,0:T(8,128)(2,1)S(1)}, bf16[128,896]{1,0:T(8,128)(2,1)S(1)}, f32[1,896]{1,0:T(1,128)S(1)}) custom-call(bf16[128,2048]{1,0:T(8,128)(2,1)S(1)} %bitcast.8, bf16[128,2048]{1,0:T(8,128)(2,1)S(1)} %bitcast.9, bf16[128,896]{1,0:T(8,128)(2,1)S(1)} %bitcast.11, f32[1,896]{1,0:T(1,128)S(1)} %reshape.22.gain_ref, ...), custom_call_target="tpu_custom_call" | custom-call | tf_op jit(solution)/shard_map/pallas_call | solution.py:547
  132.8 0.6 reduce
  133.4 0.8 copy.13
  134.2 0.7 copy.14
  (2 shorter events, 0.0 us)
Async XLA Ops:
  0.6 0.7 copy-start.4
  0.6 0.8 copy-start.5
  0.7 0.8 copy-start.3
  1.5 1.6 %copy-start = (bf16[1,128,2048]{2,1,0:T(8,128)(2,1)S(1)}, bf16[1,128,2048]{2,1,0:T(8,128)(2,1)}, u32[]{:S(2)}) copy-start(bf16[1,128,2048]{2,1,0:T(8,128)(2,1)} %param.7) | copy-start | bytes 1572868
  1.5 1.6 %copy-start.1 = (bf16[1,128,2048]{2,1,0:T(8,128)(2,1)S(1)}, bf16[1,128,2048]{2,1,0:T(8,128)(2,1)}, u32[]{:S(2)}) copy-start(bf16[1,128,2048]{2,1,0:T(8,128)(2,1)} %param.8) | copy-start | bytes 1572868
  1.5 1.6 %copy-start.2 = (bf16[1,16,8,896]{3,2,1,0:T(8,128)(2,1)S(1)}, bf16[1,16,8,896]{3,2,1,0:T(8,128)(2,1)}, u32[]{:S(2)}) copy-start(bf16[1,16,8,896]{3,2,1,0:T(8,128)(2,1)} %param.9) | copy-start | bytes 688132

commit v3 on v2

--- a/solution.py
+++ b/solution.py
@@ -14,6 +14,7 @@
 Y_SIZE = 4
 CHUNKS = 2
 X_CORES = 2
+MAIN = 4
 CAP = 3
 
 MESH = pl.DeviceIdType.MESH
@@ -34,7 +35,8 @@
         self.z = lax.rem(me, nz)
         self.up = self.at(self.y, lax.rem(self.z + 1, nz))
         self.down = self.at(self.y, lax.rem(self.z + nz - 1, nz))
-        self.across = [lax.rem(self.y + j, ny) for j in range(1, ny)]
+        order = sorted(range(1, ny), key=lambda j: -min(j, ny - j))
+        self.across = [lax.rem(self.y + j, ny) for j in order]
 
     def at(self, y, z):
         return {"seq": y * self.nz + z}
@@ -50,6 +52,7 @@
         device_id_type=MESH,
     )
 
+
 MINOR = (((1,), (1,)), ((), ()))
 MAJOR = (((0,), (0,)), ((), ()))
 
@@ -64,12 +67,13 @@
 
 def kernel(
     ny, nz, nb,
-    q_ref, do_ref, states_ref, gain_ref, kv_ref, ids_ref,
+    q_hbm, do_hbm, states_ref, gain_ref, kv_hbm, owners_ref, slots_ref,
     dq_ref, out_ref, gain_out_ref,
     ring, tabs, tab, pos, outs, recv, acc, mine, grad_rows, ids, ids_before, weight,
-    back, sums_in, sums_out, added, own, by_batch, by_y, by_z,
+    back, sums_in, sums_out, added, own, by_batch, by_y, by_z, q_ref, do_ref, kv_ref,
     ring_send, ring_recv, y_send, y_recv, tab_send, tab_recv, id_send, id_recv, w_send, w_recv,
     sum_send, sum_recv, back_send, back_recv, b_send, b_recv, gy_send, gy_recv, z_send, z_recv,
+    in_sems,
 ):
     half = nz // 2
     place = Place(ny, nz)
@@ -80,6 +84,8 @@
     wide = outs.shape[1]
     block = wide // ny
     wanted = acc.shape[0]
+    pieces = 2 * CAP
+    length = block // pieces
     steps_pad = tab.shape[0]
     count = ny * nz
     following = {"seq": lax.rem(me + 1, count)}
@@ -109,15 +115,34 @@
             place.down if way == 0 else place.up,
         )
 
+
+    main, rest = MAIN * length, block - MAIN * length
+
     def exchange(into, send, arrived, slot, j):
         there = place.across[j]
+        first, size, row = 0, block, slot
+        if isinstance(slot, int) and slot == half - 1:
+            size = main
+        elif isinstance(slot, int) and slot == half:
+            first, size, row = ny * main, rest, half - 1
         return remote(
-            outs.at[slot, pl.ds(there * block, block)],
-            into.at[slot, pl.ds(y * block, block)],
+            outs.at[row, pl.ds(first + there * size, size)],
+            into.at[row, pl.ds(first + y * size, size)],
             send.at[slot, j],
             arrived.at[slot, j],
             place.at(there, z),
         )
+
+    def keep(into, slot):
+        if isinstance(slot, int) and slot == half - 1:
+            here = pl.ds(y * main, main)
+            into[half - 1, here] = outs[half - 1, here]
+        elif isinstance(slot, int) and slot == half:
+            here = pl.ds(ny * main + y * rest, rest)
+            into[half - 1, here] = outs[half - 1, here]
+        else:
+            here = pl.ds(y * block, block)
+            into[slot, here] = outs[slot, here]
 
     def across(slot, j):
         return exchange(recv, y_send, y_recv, slot, j)
@@ -132,7 +157,7 @@
         )
 
 
-    depth = kv_ref.shape[0]
+    depth = kv_hbm.shape[0]
     cut = (depth + 31) // 32 * 16
     weight_parts = ((0, cut), (cut, depth - cut))
 
@@ -145,7 +170,7 @@
             device = (right, left, None, sibling, sibling, sibling, sibling)[channel]
         there = weight.at[pl.ds(pl.multiple_of(shard * depth + first, 16), size)]
         return remote(
-            kv_ref.at[pl.ds(first, size)] if channel in (0, 1, 3) else there,
+            there,
             there,
             w_send.at[channel, number],
             w_recv.at[channel, number],
@@ -208,10 +233,20 @@
         return result
 
 
+    kv_in = pltpu.make_async_copy(kv_hbm, kv_ref, in_sems.at[0])
+    q_in = pltpu.make_async_copy(q_hbm, q_ref, in_sems.at[1])
+    do_in = pltpu.make_async_copy(do_hbm, do_ref, in_sems.at[2])
+    for copy in (kv_in, q_in, do_in):
+        copy.start()
+
+    gain = gain_ref[...].reshape(1, width)
     values = states_ref[...].astype(F32)
-    ring[half - 1, :rows] = (values * inverse_norm(values) * gain_ref[...]).astype(BF16)
+    ring[half - 1, :rows] = (values * inverse_norm(values) * gain).astype(BF16)
     ids[...] = jnp.zeros_like(ids)
-    ids[: ids_ref.shape[0], : ids_ref.shape[1]] = ids_ref[...]
+    group = owners_ref.shape[2]
+    for i in range(owners_ref.shape[1]):
+        ids[0:1, i * group : (i + 1) * group] = owners_ref[0, i : i + 1]
+        ids[1:2, i * group : (i + 1) * group] = slots_ref[0, i : i + 1]
 
     barrier = pltpu.get_barrier_semaphore()
     peers = (
@@ -229,19 +264,9 @@
     for chunk in range(CHUNKS):
         for way in range(2):
             forward(0, way, chunk).start()
-    for number in range(2):
-        weight_copy(0, number).start()
-        weight_copy(1, 1 - number).start()
-    for number in range(2):
-        weight_copy(3, number).start()
-    acc[...] = jnp.zeros_like(acc)
-    weight[pl.ds(pl.multiple_of(b * depth, 16), depth)] = kv_ref[...]
-
-
-    pieces = 2 * CAP
-    length = block // pieces
-    own_count = ids_ref.shape[1]
-    group = own_count // 2
+
+
+    own_count = 2 * group
     request_count = own_count + group
     ids_copy.wait()
     lane = iota(ids.shape, 1)
@@ -264,18 +289,34 @@
     ahead = jnp.where(ahead < 0, ahead + nz, ahead)
     way = jnp.where(ahead >= half, 1, 0)
     distance = jnp.where(ahead == 0, half, jnp.where(ahead > half, nz - ahead, ahead))
-    piece = way * CAP + rank
+    piece = (1 - way) * CAP + rank
     cell = jnp.where(owner >= 0, column * steps_pad + distance - 1, -1)
-    number = jnp.where(owner >= 0, ((distance - 1) * ny + column) * pieces + piece, -1)
+    last = jnp.where(
+        piece < MAIN, column * MAIN + piece, ny * MAIN + column * (pieces - MAIN) + piece - MAIN
+    )
+    number = jnp.where(distance == half, last, column * pieces + piece)
+    number = jnp.where(owner >= 0, (distance - 1) * ny * pieces + number, -1)
     value = way * rows + slot_id * length + 1
 
     table_rows, table_lanes = ny * steps_pad, tab.shape[1]
     lanes_of = (table_lanes, lane.shape[1])
-    row = iota(lanes_of, 0) - y * block
-    row_piece = jnp.where((row >= 0) & (row < block), lax.div(row, length), -1)
-    chosen = jnp.where(row_piece == piece, value, 0).astype(F32).astype(BF16)
     cells = one_hot(iota((table_rows, lane.shape[1]), 0) == cell)
-    found = lax.dot_general(cells, chosen, MINOR, preferred_element_type=F32).astype(jnp.int32)
+
+    def found_at(first, size, first_piece):
+        row = iota(lanes_of, 0) - (first + y * size)
+        inside = (row >= 0) & (row < size)
+        return jnp.where(inside, lax.div(row, length) + first_piece, -1)
+
+    def found_by(row_piece):
+        chosen = jnp.where(row_piece == piece, value, 0).astype(F32).astype(BF16)
+        return lax.dot_general(cells, chosen, MINOR, preferred_element_type=F32)
+
+    whole = found_by(found_at(0, block, 0))
+    cut_in_two = found_by(
+        jnp.maximum(found_at(0, main, 0), found_at(ny * main, rest, MAIN))
+    )
+    step_of = lax.rem(iota((table_rows, table_lanes), 0), steps_pad)
+    found = jnp.where(step_of == half - 1, cut_in_two, whole).astype(jnp.int32)
     token = lax.rem(iota((table_rows, table_lanes), 1), length)
     table = jnp.where(found > 0, found + token, 0)
     for j in range(ny):
@@ -291,13 +332,21 @@
     token = lax.rem(iota(placed.shape, 1), length)
     pos[...] = jnp.where(placed >= 0, placed * length + token, -1)
 
-    for j in range(ny - 1):
-        table_copy(j).wait()
-    asked = tabs[0]
-    for j in range(1, ny):
-        asked = asked + tabs[j]
-    tab[...] = asked
-
+    acc[...] = jnp.zeros_like(acc)
+    kv_in.wait()
+    own_shard = pl.ds(pl.multiple_of(b * depth, 16), depth)
+    weight[own_shard, : kv_ref.shape[2]] = kv_ref[:, 0, :]
+    weight[own_shard, kv_ref.shape[2] :] = kv_ref[:, 1, :]
+    for number in range(2):
+        weight_copy(0, number).start()
+        weight_copy(1, 1 - number).start()
+    for number in range(2):
+        weight_copy(3, number).start()
+
+
+    def selected_in(rows_there, first, size):
+        row = tab[half - 1 : half, first : first + size]
+        return one_hot(iota((rows_there, size), 0) + 1 == row)
 
     def selected(slot):
         row = tab[pl.ds(slot, 1), :wide]
@@ -306,20 +355,36 @@
     def placing(slot):
         return one_hot(iota((wide, wanted), 0) + slot * wide == pos[0:1, :wanted])
 
+    def pick_by(select, shards):
+        return lax.dot_general(select, shards, MAJOR, preferred_element_type=F32).astype(BF16)
+
     def pick(slot):
-        outs[slot] = lax.dot_general(
-            selected(slot), ring[slot], MAJOR, preferred_element_type=F32
-        ).astype(BF16)
+        if isinstance(slot, int) and slot == half:
+            outs[half - 1, ny * main :] = pick_by(
+                selected_in(rows, ny * main, ny * rest), ring[half - 1, :rows]
+            )
+        elif isinstance(slot, int) and slot == half - 1:
+            outs[half - 1, : ny * main] = pick_by(
+                selected_in(2 * rows, 0, ny * main), ring[half - 1]
+            )
+        else:
+            outs[slot] = pick_by(selected(slot), ring[slot])
         for j in range(ny - 1):
             across(slot, j).start()
-        recv[slot, pl.ds(y * block, block)] = outs[slot, pl.ds(y * block, block)]
+        keep(recv, slot)
 
     def take(slot):
         for j in range(ny - 1):
             across(slot, j).wait_recv()
+            if isinstance(slot, int) and slot == half - 1:
+                across(half, j).wait_recv()
         acc[...] += lax.dot_general(placing(slot), recv[slot], MAJOR, preferred_element_type=F32)
 
     def near(slot, last):
+        hand_on(slot, last)
+        pick(slot)
+
+    def hand_on(slot, last):
         for chunk in range(CHUNKS):
             for way in range(2):
                 forward(slot, way, chunk).wait_recv()
@@ -327,10 +392,17 @@
                     forward(slot + 1, way, chunk).start()
                 elif way == chunk:
                     forward(half - 1, way, chunk).start()
-        pick(slot)
 
     services = {2: weights_one, 4: weights_two}
-    near(0, half == 2)
+    hand_on(0, half == 2)
+    for j in range(ny - 1):
+        table_copy(j).wait()
+    asked = tabs[0]
+    for j in range(1, ny):
+        asked = asked + tabs[j]
+    tab[...] = asked
+    pick(half)
+    pick(0)
     if half > 2:
 
         @pl.loop(1, half - 2)
@@ -372,8 +444,12 @@
                     place.down if way == 0 else place.up,
                 ).wait_send()
 
-    @pl.loop(0, half)
+    @pl.loop(0, half - 1)
     def _(slot):
+        for j in range(ny - 1):
+            across(slot, j).wait_send()
+
+    for slot in (half - 1, half):
         for j in range(ny - 1):
             across(slot, j).wait_send()
 
@@ -382,14 +458,16 @@
             weight_copy(channel, number).wait_send()
 
 
+    q_in.wait()
+    do_in.wait()
     tokens = q_ref.shape[0]
     scaling = 1.0 / math.sqrt(HEAD_DIM)
-    turn = lax.div(iota((tokens, wanted), 0) + 1, GROUP)
-    key_group = lax.div(iota((tokens, wanted), 1), GROUP)
+    turn = lax.div(iota((wanted, tokens), 1) + 1, GROUP)
+    key_group = lax.div(iota((wanted, tokens), 0), GROUP)
     mask = lax.rem(turn + 2, 3) == key_group
     mask = mask & ((turn > 0) | (me > 0))
     pages = mine[...]
-    heads_wide = 2 * HEAD_DIM
+    heads_wide = min(8 * HEAD_DIM, q_ref.shape[1])
     steps = q_ref.shape[1] // heads_wide
     acc[...] = jnp.zeros_like(acc)
 
@@ -408,17 +486,17 @@
             columns = slice(head * HEAD_DIM, (head + 1) * HEAD_DIM)
             query, grad = queries[:, columns], grads[:, columns]
             key, val = key_all[:, columns], value_all[:, columns]
-            scores = lax.dot_general(query, key, MINOR, preferred_element_type=F32) * scaling
-            weights = jnp.where(mask, jnp.exp(jnp.where(mask, scores, 0.0)), 0.0)
-            over = jnp.sum(weights, axis=-1, keepdims=True)
-            probability = weights / jnp.where(over == 0.0, 1.0, over)
-            grad_probability = lax.dot_general(grad, val, MINOR, preferred_element_type=F32)
-            delta = jnp.sum(probability * grad_probability, axis=-1, keepdims=True)
+            scores = lax.dot_general(key, query, MINOR, preferred_element_type=F32) * scaling
+            weights = jnp.where(mask, jnp.exp(scores), 0.0)
+            over = jnp.sum(weights, axis=0, keepdims=True)
+            probability = weights * (1.0 / jnp.where(over == 0.0, 1.0, over))
+            grad_probability = lax.dot_general(val, grad, MINOR, preferred_element_type=F32)
+            delta = jnp.sum(probability * grad_probability, axis=0, keepdims=True)
             grad_scores = (probability * (grad_probability - delta) * scaling).astype(BF16)
             low = probability.astype(BF16)
-            query_grads.append(jnp.dot(grad_scores, key, preferred_element_type=F32))
-            key_grads.append(lax.dot_general(grad_scores, query, MAJOR, preferred_element_type=F32))
-            value_grads.append(lax.dot_general(low, grad, MAJOR, preferred_element_type=F32))
+            query_grads.append(lax.dot_general(grad_scores, key, MAJOR, preferred_element_type=F32))
+            key_grads.append(jnp.dot(grad_scores, query, preferred_element_type=F32))
+            value_grads.append(jnp.dot(low, grad, preferred_element_type=F32))
         dq_ref[:, here] = jnp.concatenate(query_grads, axis=1).astype(BF16)
         key_grad = jnp.concatenate(key_grads, axis=1).astype(BF16)
         value_grad = jnp.concatenate(value_grads, axis=1).astype(BF16)
@@ -433,12 +511,34 @@
         outs[slot] = jnp.dot(placing(slot), grad_rows[...], preferred_element_type=F32).astype(BF16)
         for j in range(ny - 1):
             return_across(slot, j).start()
-        back[slot, pl.ds(y * block, block)] = outs[slot, pl.ds(y * block, block)]
+        keep(back, slot)
+
+    def scatter_rest():
+        for j in range(ny - 1):
+            return_across(half, j).start()
+        keep(back, half)
+
+    def gather_by(select, blocks):
+        return jnp.dot(select, blocks, preferred_element_type=F32)
 
     def gather(slot):
         for j in range(ny - 1):
             return_across(slot, j).wait_recv()
-        added[...] = jnp.dot(selected(slot), back[slot], preferred_element_type=F32)
+        added[...] = gather_by(selected(slot), back[slot])
+
+    def gather_far():
+        for j in range(ny - 1):
+            return_across(half - 1, j).wait_recv()
+        added[...] = gather_by(
+            selected_in(2 * rows, 0, ny * main), back[half - 1, : ny * main]
+        )
+
+    def gather_rest():
+        for j in range(ny - 1):
+            return_across(half, j).wait_recv()
+        own[...] += gather_by(
+            selected_in(rows, ny * main, ny * rest), back[half - 1, ny * main :]
+        )
 
     def relay(distance, first):
         gather(distance - 1)
@@ -455,7 +555,7 @@
     def gain_one():
         lanes = width // 128
         products = jnp.sum(grad_rows[...].astype(F32) * mine[...].astype(F32), axis=0, keepdims=True)
-        products = products / gain_ref[...]
+        products = products / gain
         by_batch[pl.ds(b, 1)] = jnp.zeros_like(by_batch[pl.ds(b, 1)])
         for i in range(lanes):
             by_batch[b, i : i + 1] = products[:, i * 128 : (i + 1) * 128]
@@ -478,14 +578,16 @@
 
     scatter(half - 1)
     scatter(half - 2)
-    gather(half - 1)
-    own[...] = added[:rows]
+    scatter_rest()
+    gain_one()
+    if half > 2:
+        scatter(half - 3)
+    gather_far()
     sums_out[half - 1, pl.ds(rows, rows)] = added[pl.ds(rows, rows)].astype(BF16)
     for way in range(2):
         pass_on(half, way, way).start()
-    gain_one()
-    if half > 2:
-        scatter(half - 3)
+    own[...] = added[:rows]
+    gather_rest()
     relay(half - 1, True)
     gain_two()
     if half > 2:
@@ -504,7 +606,7 @@
         z_copy(j).wait()
     result = total(by_z)
     for i in range(width // 128):
-        gain_out_ref[:, i * 128 : (i + 1) * 128] = result[i : i + 1]
+        gain_out_ref[i * 128 : (i + 1) * 128] = result[i]
 
     for chunk in range(CHUNKS):
         here = pl.ds(chunk * part, part)
@@ -514,7 +616,7 @@
         normed_grad = normed_grad + sums_in[0, pl.ds(rows + chunk * part, part)].astype(F32)
         values = states_ref[here].astype(F32)
         inverse = inverse_norm(values)
-        scaled = normed_grad * gain_ref[...]
+        scaled = normed_grad * gain
         inner = jnp.mean(scaled * values, axis=-1, keepdims=True)
         out_ref[here] = (
             inverse * scaled - values * (inverse * inverse * inverse * inner)
@@ -529,8 +631,12 @@
             for chunk in range(CHUNKS):
                 pass_on(distance, way, chunk).wait_send()
 
-    @pl.loop(0, half)
+    @pl.loop(0, half - 1)
     def _(slot):
+        for j in range(ny - 1):
+            return_across(slot, j).wait_send()
+
+    for slot in (half - 1, half):
         for j in range(ny - 1):
             return_across(slot, j).wait_send()
 
@@ -542,16 +648,18 @@
     wanted = owners.shape[1] * owners.shape[2] * 3 // 2 * length
     wide = ny * 2 * CAP * length
     table = (max(8, half), wide + -wide % 128)
-    ids = jnp.stack([owners.reshape(-1), slots.reshape(-1)])
     dma = pltpu.SemaphoreType.DMA
     query_grad, state_grad, gain_grad = pl.pallas_call(
         functools.partial(kernel, ny, nz, nb),
         out_shape=(
             jax.ShapeDtypeStruct((tokens, width), BF16),
             jax.ShapeDtypeStruct((rows, enc), BF16),
-            jax.ShapeDtypeStruct((1, enc), F32),
+            jax.ShapeDtypeStruct((enc,), F32),
         ),
-        in_specs=[pl.BlockSpec(memory_space=VMEM)] * 6,
+        in_specs=[
+            pl.BlockSpec(memory_space=VMEM if inside else pl.ANY)
+            for inside in (False, False, True, True, False, True, True)
+        ],
         out_specs=(pl.BlockSpec(memory_space=VMEM),) * 3,
         scratch_shapes=[
             VMEM((half, 2 * rows, enc), BF16),
@@ -574,28 +682,31 @@
             VMEM((nb, 8, 128), F32),
             VMEM((ny, 8, 128), F32),
             VMEM((nz, 8, 128), F32),
+            VMEM((tokens, width), BF16),
+            VMEM((tokens, width), BF16),
+            VMEM(kv_weight.shape, BF16),
             dma((half, 2, CHUNKS)), dma((half, 2, CHUNKS)),
-            dma((half, ny - 1)), dma((half, ny - 1)),
+            dma((half + 1, ny - 1)), dma((half + 1, ny - 1)),
             dma((ny - 1,)), dma((ny - 1,)),
             dma, dma,
             dma((7, 2)), dma((7, 2)),
             dma((half, 2, CHUNKS)), dma((half, 2, CHUNKS)),
-            dma((half, ny - 1)), dma((half, ny - 1)),
+            dma((half + 1, ny - 1)), dma((half + 1, ny - 1)),
             dma((nb - 1,)), dma((nb - 1,)),
             dma((ny - 1,)), dma((ny - 1,)),
             dma((nz - 1,)), dma((nz - 1,)),
+            dma((3,)),
         ],
         compiler_params=pltpu.CompilerParams(
-            collective_id=1, has_side_effects=True, vmem_limit_bytes=48 << 20
+            collective_id=1, has_side_effects=True, vmem_limit_bytes=54 << 20
         ),
     )(
-        queries[0], out_grad[0], states.reshape(rows, enc), gain.reshape(1, enc),
-        kv_weight.reshape(-1, 2 * width), ids,
+        queries[0], out_grad[0], states.reshape(rows, enc), gain, kv_weight, owners, slots,
     )
     return (
         query_grad[None],
         state_grad.reshape(1, held, length, enc),
-        gain_grad.reshape(enc),
+        gain_grad,
     )
 
 

time: 136 us -> 130 us (0.956)
  Pallas kernels: 130 us -> 126 us
    pallas_call x1, Pallas kernels: 130 us -> 126 us  [on_device(): pl.pallas_call(functools.partial(kernel, ny, nz, nb), out_shape=(jax.Shap...]
    unnamed x15 -> x7, local copies, waits for them, and re-layouts: 3.74 us -> 3.21 us
where the time goes in v3:
time: 130 us
  Pallas kernels  126 us (97%)
  local copies, waits for them, and re-layouts  3.21 us (2%)
    pallas_call x1, Pallas kernels, on_device(): pl.pallas_call(functools.partial(kernel, ny, nz, nb), out_shape=(jax.Shap...  126 us
    unnamed x7, local copies, waits for them, and re-layouts  3.21 us

profile of v3, /device:TPU:6, one launch (start us, length us, event | category | flops | bytes accessed | tf_op | source)
XLA Modules:
  0.0 130.0 jit_solution(15337878915545317114)
XLA Ops:
  0.6 126.1 %shard_map.94 = (bf16[128,2048]{1,0:T(8,128)(2,1)}, bf16[128,896]{1,0:T(8,128)(2,1)}, f32[896]{0:T(1024)}) custom-call(bf16[128,2048]{1,0:T(8,128)(2,1)} %bitcast.5, bf16[128,2048]{1,0:T(8,128)(2,1)} %bitcast.6, bf16[128,896]{1,0:T(8,128)(2,1)} %bitcast.8, f32[896]{0:T(1024)} %gain_ref.1, bf16[112,2,2048]{2,1,0:T(2,128)(2,1)} %kv_hbm.1, ...), custom_call_target="tpu_custom_call" | custom-call | tf_op jit(solution)/shard_map/pallas_call | solution.py:652
  126.8 0.0 copy-start
  126.8 1.9 %copy.13 = bf16[1,128,2048]{2,1,0:T(8,128)(2,1)} copy(bf16[1,128,2048]{2,1,0:T(8,128)(2,1)} %bitcast.7) | data formatting | bytes 1048576
  128.7 0.0 copy-done
  128.7 0.0 copy-start.1
  128.7 0.7 copy.14
  129.4 0.0 copy-done.1
  129.4 0.6 copy.15
Async XLA Ops:
  126.8 1.9 %copy-start = (bf16[128,896]{1,0:T(8,128)(2,1)S(1)}, bf16[128,896]{1,0:T(8,128)(2,1)}, u32[]{:S(2)}) copy-start(bf16[128,896]{1,0:T(8,128)(2,1)} %get-tuple-element.7) | copy-start | bytes 688132
  128.7 0.7 copy-start.1

commit v4 on v3

--- a/solution.py
+++ b/solution.py
@@ -69,10 +69,10 @@
     ny, nz, nb,
     q_hbm, do_hbm, states_ref, gain_ref, kv_hbm, owners_ref, slots_ref,
     dq_ref, out_ref, gain_out_ref,
-    ring, tabs, tab, pos, outs, recv, acc, mine, grad_rows, ids, ids_before, weight,
-    back, sums_in, sums_out, added, own, by_batch, by_y, by_z, q_ref, do_ref, kv_ref,
+    ring, tabs, tab, pos, outs, recv, acc, mine, grad_rows, keys_kept, scores_kept, ids, ids_before, weight,
+    back_outs, back, sums_in, sums_out, added, own, by_x, by_core, by_y, by_z, q_ref, do_ref, kv_ref,
     ring_send, ring_recv, y_send, y_recv, tab_send, tab_recv, id_send, id_recv, w_send, w_recv,
-    sum_send, sum_recv, back_send, back_recv, b_send, b_recv, gy_send, gy_recv, z_send, z_recv,
+    sum_send, sum_recv, back_send, back_recv, x_send, x_recv, core_send, core_recv, gy_send, gy_recv, z_send, z_recv,
     in_sems,
 ):
     half = nz // 2
@@ -90,7 +90,7 @@
     count = ny * nz
     following = {"seq": lax.rem(me + 1, count)}
     preceding = {"seq": lax.rem(me + count - 1, count)}
-    b_peers = [lax.rem(b + j, nb) for j in range(1, nb)]
+    x_peers = [lax.rem(b + j * X_CORES, nb) for j in range(1, nb // X_CORES)]
     z_peers = [lax.rem(z + j, nz) for j in range(1, nz)]
     core = lax.rem(b, X_CORES)
     right = lax.rem(b + X_CORES, nb)
@@ -110,7 +110,7 @@
         return remote(
             src,
             dst,
-            ring_send.at[slot, way, chunk],
+            ring_send,
             ring_recv.at[slot, way, chunk],
             place.down if way == 0 else place.up,
         )
@@ -118,7 +118,7 @@
 
     main, rest = MAIN * length, block - MAIN * length
 
-    def exchange(into, send, arrived, slot, j):
+    def exchange(out, into, send, arrived, slot, j):
         there = place.across[j]
         first, size, row = 0, block, slot
         if isinstance(slot, int) and slot == half - 1:
@@ -126,34 +126,34 @@
         elif isinstance(slot, int) and slot == half:
             first, size, row = ny * main, rest, half - 1
         return remote(
-            outs.at[row, pl.ds(first + there * size, size)],
+            out.at[row, pl.ds(first + there * size, size)],
             into.at[row, pl.ds(first + y * size, size)],
-            send.at[slot, j],
+            send,
             arrived.at[slot, j],
             place.at(there, z),
         )
 
-    def keep(into, slot):
+    def keep(out, into, slot):
         if isinstance(slot, int) and slot == half - 1:
             here = pl.ds(y * main, main)
-            into[half - 1, here] = outs[half - 1, here]
+            into[half - 1, here] = out[half - 1, here]
         elif isinstance(slot, int) and slot == half:
             here = pl.ds(ny * main + y * rest, rest)
-            into[half - 1, here] = outs[half - 1, here]
+            into[half - 1, here] = out[half - 1, here]
         else:
             here = pl.ds(y * block, block)
-            into[slot, here] = outs[slot, here]
+            into[slot, here] = out[slot, here]
 
     def across(slot, j):
-        return exchange(recv, y_send, y_recv, slot, j)
+        return exchange(outs, recv, y_send, y_recv, slot, j)
 
     def return_across(slot, j):
-        return exchange(back, back_send, back_recv, slot, j)
+        return exchange(back_outs, back, back_send, back_recv, slot, j)
 
     def table_copy(j):
         there = place.across[j]
         return remote(
-            tabs.at[ny + there], tabs.at[y], tab_send.at[j], tab_recv.at[j], place.at(there, z)
+            tabs.at[ny + there], tabs.at[y], tab_send, tab_recv, place.at(there, z)
         )
 
 
@@ -172,12 +172,15 @@
         return remote(
             there,
             there,
-            w_send.at[channel, number],
+            w_send,
             w_recv.at[channel, number],
             {"batch": device},
         )
 
     def weights_one():
+        answer()
+        for number in range(2):
+            weight_copy(3, number).start()
         weight_copy(0, 0).wait_recv()
         weight_copy(2, 0).start()
         weight_copy(4, 0).start()
@@ -205,25 +208,35 @@
         return remote(
             part_of(sums_out, distance - 1, 1 if far else way, chunk),
             part_of(sums_in, distance - 1, way, chunk),
-            sum_send.at[distance - 1, way, chunk],
+            sum_send,
             sum_recv.at[distance - 1, way, chunk],
             place.up if way == 0 else place.down,
         )
 
-
-    def b_copy(j):
-        return remote(
-            by_batch.at[b], by_batch.at[b], b_send.at[j], b_recv.at[j], {"batch": b_peers[j]}
+    def all_of(ref, send, arrived):
+        return remote(ref, ref, send, arrived, place.up)
+
+
+    x = lax.div(b, X_CORES)
+
+    def x_copy(j):
+        return remote(
+            by_x.at[x], by_x.at[x], x_send, x_recv, {"batch": x_peers[j]}
+        )
+
+    def core_copy():
+        return remote(
+            by_core.at[core], by_core.at[core], core_send, core_recv, {"batch": sibling}
         )
 
     def gy_copy(j):
         return remote(
-            by_y.at[y], by_y.at[y], gy_send.at[j], gy_recv.at[j], place.at(place.across[j], z)
+            by_y.at[y], by_y.at[y], gy_send, gy_recv, place.at(place.across[j], z)
         )
 
     def z_copy(j):
         return remote(
-            by_z.at[z], by_z.at[z], z_send.at[j], z_recv.at[j], place.at(y, z_peers[j])
+            by_z.at[z], by_z.at[z], z_send, z_recv, place.at(y, z_peers[j])
         )
 
     def total(ref):
@@ -249,15 +262,32 @@
         ids[1:2, i * group : (i + 1) * group] = slots_ref[0, i : i + 1]
 
     barrier = pltpu.get_barrier_semaphore()
+
+    def tell(device):
+        pl.semaphore_signal(barrier, inc=1, device_id=device, device_id_type=MESH)
+
     peers = (
-        [{"batch": peer} for peer in b_peers]
+        [place.up, place.down, preceding]
         + [place.at(there, z) for there in place.across]
-        + [place.at(y, there) for there in z_peers]
-        + [preceding]
+        + [{"batch": peer} for peer in x_peers]
     )
     for peer in peers:
-        pl.semaphore_signal(barrier, inc=1, device_id=peer, device_id_type=MESH)
-    pl.semaphore_wait(barrier, len(peers))
+        tell(peer)
+
+    @pl.when(core == 0)
+    def _():
+        pl.semaphore_wait(barrier, len(peers))
+
+    @pl.when(core == 1)
+    def _():
+        pl.semaphore_wait(barrier, len(peers) + 1)
+
+    tell({"batch": sibling})
+
+    def answer():
+        @pl.when(core == 0)
+        def _():
+            pl.semaphore_wait(barrier, 1)
 
     ids_copy = remote(ids, ids_before, id_send, id_recv, following)
     ids_copy.start()
@@ -340,8 +370,6 @@
     for number in range(2):
         weight_copy(0, number).start()
         weight_copy(1, 1 - number).start()
-    for number in range(2):
-        weight_copy(3, number).start()
 
 
     def selected_in(rows_there, first, size):
@@ -371,7 +399,7 @@
             outs[slot] = pick_by(selected(slot), ring[slot])
         for j in range(ny - 1):
             across(slot, j).start()
-        keep(recv, slot)
+        keep(outs, recv, slot)
 
     def take(slot):
         for j in range(ny - 1):
@@ -395,8 +423,7 @@
 
     services = {2: weights_one, 4: weights_two}
     hand_on(0, half == 2)
-    for j in range(ny - 1):
-        table_copy(j).wait()
+    all_of(tabs.at[pl.ds(0, ny - 1)], tab_send, tab_recv).wait()
     asked = tabs[0]
     for j in range(1, ny):
         asked = asked + tabs[j]
@@ -429,34 +456,6 @@
     take(half - 1)
     mine[...] = acc[...].astype(BF16)
 
-    for way in range(2):
-        forward(half - 1, way, way).wait_send()
-
-    @pl.loop(0, half - 1)
-    def _(slot):
-        for way in range(2):
-            for chunk in range(CHUNKS):
-                remote(
-                    ring_part(0, way, chunk),
-                    ring_part(0, way, chunk),
-                    ring_send.at[slot, way, chunk],
-                    ring_recv.at[slot, way, chunk],
-                    place.down if way == 0 else place.up,
-                ).wait_send()
-
-    @pl.loop(0, half - 1)
-    def _(slot):
-        for j in range(ny - 1):
-            across(slot, j).wait_send()
-
-    for slot in (half - 1, half):
-        for j in range(ny - 1):
-            across(slot, j).wait_send()
-
-    for channel in range(7):
-        for number in range(2):
-            weight_copy(channel, number).wait_send()
-
 
     q_in.wait()
     do_in.wait()
@@ -481,7 +480,8 @@
         key_all = jnp.dot(pages, key_weight, preferred_element_type=F32).astype(BF16)
         value_all = jnp.dot(pages, value_weight, preferred_element_type=F32).astype(BF16)
         queries, grads = q_ref[:, here], do_ref[:, here]
-        query_grads, key_grads, value_grads = [], [], []
+        key_grads, value_grads = [], []
+        keys_kept[:, here] = key_all
         for head in range(heads_wide // HEAD_DIM):
             columns = slice(head * HEAD_DIM, (head + 1) * HEAD_DIM)
             query, grad = queries[:, columns], grads[:, columns]
@@ -494,10 +494,9 @@
             delta = jnp.sum(probability * grad_probability, axis=0, keepdims=True)
             grad_scores = (probability * (grad_probability - delta) * scaling).astype(BF16)
             low = probability.astype(BF16)
-            query_grads.append(lax.dot_general(grad_scores, key, MAJOR, preferred_element_type=F32))
+            scores_kept[:, pl.ds(here.start + head * HEAD_DIM, HEAD_DIM)] = grad_scores
             key_grads.append(jnp.dot(grad_scores, query, preferred_element_type=F32))
             value_grads.append(jnp.dot(low, grad, preferred_element_type=F32))
-        dq_ref[:, here] = jnp.concatenate(query_grads, axis=1).astype(BF16)
         key_grad = jnp.concatenate(key_grads, axis=1).astype(BF16)
         value_grad = jnp.concatenate(value_grads, axis=1).astype(BF16)
         change = lax.dot_general(key_grad, key_weight, MINOR, preferred_element_type=F32)
@@ -506,17 +505,23 @@
 
     grad_rows[...] = acc[...].astype(BF16)
 
+    def query_grad(head):
+        here = pl.ds(pl.multiple_of(head * HEAD_DIM, HEAD_DIM), HEAD_DIM)
+        dq_ref[:, here] = lax.dot_general(
+            scores_kept[:, here], keys_kept[:, here], MAJOR, preferred_element_type=F32
+        ).astype(BF16)
+
 
     def scatter(slot):
-        outs[slot] = jnp.dot(placing(slot), grad_rows[...], preferred_element_type=F32).astype(BF16)
+        back_outs[slot] = jnp.dot(placing(slot), grad_rows[...], preferred_element_type=F32).astype(BF16)
         for j in range(ny - 1):
             return_across(slot, j).start()
-        keep(back, slot)
+        keep(back_outs, back, slot)
 
     def scatter_rest():
         for j in range(ny - 1):
             return_across(half, j).start()
-        keep(back, half)
+        keep(back_outs, back, half)
 
     def gather_by(select, blocks):
         return jnp.dot(select, blocks, preferred_element_type=F32)
@@ -552,26 +557,44 @@
                 sums_out[distance - 1, here] = total_here.astype(BF16)
                 pass_on(distance, way, chunk).start()
 
+    def pass_sent(ref, send):
+        every = ref.at[pl.ds(0, half - 1)]
+        all_of(every, send, send).wait_send()
+        last = ref.at[half - 1, pl.ds(0, rows)]
+        all_of(last, send, send).wait_send()
+
+    def across_sent(ref, send):
+        every = ref.at[:, pl.ds(0, wide - block)]
+        all_of(every, send, send).wait_send()
+
+    def fetch_sent():
+        pass_sent(ring, ring_send)
+        across_sent(outs, y_send)
+        all_of(weight.at[pl.ds(0, 7 * depth)], w_send, w_send).wait_send()
+
     def gain_one():
         lanes = width // 128
         products = jnp.sum(grad_rows[...].astype(F32) * mine[...].astype(F32), axis=0, keepdims=True)
         products = products / gain
-        by_batch[pl.ds(b, 1)] = jnp.zeros_like(by_batch[pl.ds(b, 1)])
+        by_x[pl.ds(x, 1)] = jnp.zeros_like(by_x[pl.ds(x, 1)])
         for i in range(lanes):
-            by_batch[b, i : i + 1] = products[:, i * 128 : (i + 1) * 128]
-        for j in range(nb - 1):
-            b_copy(j).start()
+            by_x[x, i : i + 1] = products[:, i * 128 : (i + 1) * 128]
+        for j in range(len(x_peers)):
+            x_copy(j).start()
 
     def gain_two():
-        for j in range(nb - 1):
-            b_copy(j).wait()
-        by_y[y] = total(by_batch)
+        all_of(by_x.at[pl.ds(0, len(x_peers))], x_send, x_recv).wait()
+        by_core[core] = total(by_x)
+        core_copy().start()
+
+    def gain_three():
+        core_copy().wait()
+        by_y[y] = total(by_core)
         for j in range(ny - 1):
             gy_copy(j).start()
 
-    def gain_three():
-        for j in range(ny - 1):
-            gy_copy(j).wait()
+    def gain_four():
+        all_of(by_y.at[pl.ds(0, ny - 1)], gy_send, gy_recv).wait()
         by_z[z] = total(by_y)
         for j in range(nz - 1):
             z_copy(j).start()
@@ -580,6 +603,7 @@
     scatter(half - 2)
     scatter_rest()
     gain_one()
+    fetch_sent()
     if half > 2:
         scatter(half - 3)
     gather_far()
@@ -590,6 +614,11 @@
     gather_rest()
     relay(half - 1, True)
     gain_two()
+    heads = q_ref.shape[1] // HEAD_DIM
+    turns = max(half - 3, 0)
+    each = heads // turns if turns else 0
+    for head in range(each * turns, heads):
+        query_grad(head)
     if half > 2:
 
         @pl.loop(0, half - 3)
@@ -597,13 +626,17 @@
             distance = half - 2 - i
             scatter(distance - 2)
             relay(distance, False)
-
-    gain_three()
+            pl.when(i == max(0, half - 6))(gain_three)
+            for head in range(each):
+                query_grad(i * each + head)
+
+    else:
+        gain_three()
+    gain_four()
     if half > 2:
         relay(1, False)
 
-    for j in range(nz - 1):
-        z_copy(j).wait()
+    all_of(by_z.at[pl.ds(0, nz - 1)], z_send, z_recv).wait()
     result = total(by_z)
     for i in range(width // 128):
         gain_out_ref[i * 128 : (i + 1) * 128] = result[i]
@@ -622,23 +655,8 @@
             inverse * scaled - values * (inverse * inverse * inverse * inner)
         ).astype(BF16)
 
-    for way in range(2):
-        pass_on(half, way, way).wait_send()
-
-    @pl.loop(1, half)
-    def _(distance):
-        for way in range(2):
-            for chunk in range(CHUNKS):
-                pass_on(distance, way, chunk).wait_send()
-
-    @pl.loop(0, half - 1)
-    def _(slot):
-        for j in range(ny - 1):
-            return_across(slot, j).wait_send()
-
-    for slot in (half - 1, half):
-        for j in range(ny - 1):
-            return_across(slot, j).wait_send()
+    pass_sent(sums_out, sum_send)
+    across_sent(back_outs, back_send)
 
 
 def on_device(ny, nz, nb, queries, out_grad, states, gain, kv_weight, owners, slots):
@@ -671,30 +689,35 @@
             VMEM((wanted, enc), F32),
             VMEM((wanted, enc), BF16),
             VMEM((wanted, enc), BF16),
+            VMEM((wanted, width), BF16),
+            VMEM((wanted, width), BF16),
             VMEM((8, 128), jnp.int32),
             VMEM((8, 128), jnp.int32),
             VMEM((enc, 2 * width), BF16),
+            VMEM((half, wide, enc), BF16),
             VMEM((half, wide, enc), BF16),
             VMEM((half, 2 * rows, enc), BF16),
             VMEM((half, 2 * rows, enc), BF16),
             VMEM((2 * rows, enc), F32),
             VMEM((rows, enc), F32),
-            VMEM((nb, 8, 128), F32),
+            VMEM((nb // X_CORES, 8, 128), F32),
+            VMEM((X_CORES, 8, 128), F32),
             VMEM((ny, 8, 128), F32),
             VMEM((nz, 8, 128), F32),
             VMEM((tokens, width), BF16),
             VMEM((tokens, width), BF16),
             VMEM(kv_weight.shape, BF16),
-            dma((half, 2, CHUNKS)), dma((half, 2, CHUNKS)),
-            dma((half + 1, ny - 1)), dma((half + 1, ny - 1)),
-            dma((ny - 1,)), dma((ny - 1,)),
+            dma, dma((half, 2, CHUNKS)),
+            dma, dma((half + 1, ny - 1)),
             dma, dma,
-            dma((7, 2)), dma((7, 2)),
-            dma((half, 2, CHUNKS)), dma((half, 2, CHUNKS)),
-            dma((half + 1, ny - 1)), dma((half + 1, ny - 1)),
-            dma((nb - 1,)), dma((nb - 1,)),
-            dma((ny - 1,)), dma((ny - 1,)),
-            dma((nz - 1,)), dma((nz - 1,)),
+            dma, dma,
+            dma, dma((7, 2)),
+            dma, dma((half, 2, CHUNKS)),
+            dma, dma((half + 1, ny - 1)),
+            dma, dma,
+            dma, dma,
+            dma, dma,
+            dma, dma,
             dma((3,)),
         ],
         compiler_params=pltpu.CompilerParams(

time: 130 us -> 126 us (0.969)
  Pallas kernels: 126 us -> 122 us
    pallas_call x1, Pallas kernels: 126 us -> 122 us  [on_device(): pl.pallas_call(functools.partial(kernel, ny, nz, nb), out_shape=(jax.Shap...]
where the time goes in v4:
time: 126 us
  Pallas kernels  122 us (97%)
  local copies, waits for them, and re-layouts  3.21 us (3%)
    pallas_call x1, Pallas kernels, on_device(): pl.pallas_call(functools.partial(kernel, ny, nz, nb), out_shape=(jax.Shap...  122 us
    unnamed x7, local copies, waits for them, and re-layouts  3.21 us

profile of v4, /device:TPU:6, one launch (start us, length us, event | category | flops | bytes accessed | tf_op | source)
XLA Modules:
  0.0 125.5 jit_solution(17367578449484792834)
XLA Ops:
  0.6 121.7 %shard_map.94 = (bf16[128,2048]{1,0:T(8,128)(2,1)}, bf16[128,896]{1,0:T(8,128)(2,1)}, f32[896]{0:T(1024)}) custom-call(bf16[128,2048]{1,0:T(8,128)(2,1)} %bitcast.5, bf16[128,2048]{1,0:T(8,128)(2,1)} %bitcast.6, bf16[128,896]{1,0:T(8,128)(2,1)} %bitcast.8, f32[896]{0:T(1024)} %gain_ref.1, bf16[112,2,2048]{2,1,0:T(2,128)(2,1)} %kv_hbm.1, ...), custom_call_target="tpu_custom_call" | custom-call | tf_op jit(solution)/shard_map/pallas_call | solution.py:670
  122.3 0.0 copy-start
  122.3 1.9 %copy.13 = bf16[1,128,2048]{2,1,0:T(8,128)(2,1)} copy(bf16[1,128,2048]{2,1,0:T(8,128)(2,1)} %bitcast.7) | data formatting | bytes 1048576
  124.2 0.0 copy-done
  124.2 0.0 copy-start.1
  124.2 0.7 copy.14
  124.9 0.0 copy-done.1
  124.9 0.6 copy.15
Async XLA Ops:
  122.3 1.9 %copy-start = (bf16[128,896]{1,0:T(8,128)(2,1)S(1)}, bf16[128,896]{1,0:T(8,128)(2,1)}, u32[]{:S(2)}) copy-start(bf16[128,896]{1,0:T(8,128)(2,1)} %get-tuple-element.7) | copy-start | bytes 688132
  124.2 0.7 copy-start.1

commit v5 on v4

--- a/solution.py
+++ b/solution.py
@@ -13,6 +13,8 @@
 EPS = 1e-06
 Y_SIZE = 4
 CHUNKS = 2
+FETCH_ORDER = ((0, 0), (1, 1), (0, 1), (1, 0))
+RETURN_ORDER = ((0, 1), (1, 0), (0, 0), (1, 1))
 X_CORES = 2
 MAIN = 4
 CAP = 3
@@ -291,9 +293,8 @@
 
     ids_copy = remote(ids, ids_before, id_send, id_recv, following)
     ids_copy.start()
-    for chunk in range(CHUNKS):
-        for way in range(2):
-            forward(0, way, chunk).start()
+    for way, chunk in FETCH_ORDER:
+        forward(0, way, chunk).start()
 
 
     own_count = 2 * group
@@ -413,13 +414,12 @@
         pick(slot)
 
     def hand_on(slot, last):
-        for chunk in range(CHUNKS):
-            for way in range(2):
-                forward(slot, way, chunk).wait_recv()
-                if not last:
-                    forward(slot + 1, way, chunk).start()
-                elif way == chunk:
-                    forward(half - 1, way, chunk).start()
+        for way, chunk in FETCH_ORDER:
+            forward(slot, way, chunk).wait_recv()
+            if not last:
+                forward(slot + 1, way, chunk).start()
+            elif way == chunk:
+                forward(half - 1, way, chunk).start()
 
     services = {2: weights_one, 4: weights_two}
     hand_on(0, half == 2)
@@ -547,15 +547,14 @@
 
     def relay(distance, first):
         gather(distance - 1)
-        for chunk in range(CHUNKS):
-            for way in range(2):
-                here = pl.ds(way * rows + chunk * part, part)
-                total_here = added[here]
-                if not first or way == chunk:
-                    pass_on(distance + 1, way, chunk).wait_recv()
-                    total_here = total_here + sums_in[distance, here].astype(F32)
-                sums_out[distance - 1, here] = total_here.astype(BF16)
-                pass_on(distance, way, chunk).start()
+        for way, chunk in RETURN_ORDER:
+            here = pl.ds(way * rows + chunk * part, part)
+            total_here = added[here]
+            if not first or way == chunk:
+                pass_on(distance + 1, way, chunk).wait_recv()
+                total_here = total_here + sums_in[distance, here].astype(F32)
+            sums_out[distance - 1, here] = total_here.astype(BF16)
+            pass_on(distance, way, chunk).start()
 
     def pass_sent(ref, send):
         every = ref.at[pl.ds(0, half - 1)]

time: 126 us -> 125 us (level)
  Pallas kernels: 122 us -> 120 us
    pallas_call x1, Pallas kernels: 122 us -> 120 us  [on_device(): pl.pallas_call(functools.partial(kernel, ny, nz, nb), out_shape=(jax.Shap...]
where the time goes in v5:
time: 125 us; the launch traced here: 124 us
  Pallas kernels  120 us (96%)
  local copies, waits for them, and re-layouts  3.21 us (3%)
    pallas_call x1, Pallas kernels, on_device(): pl.pallas_call(functools.partial(kernel, ny, nz, nb), out_shape=(jax.Shap...  120 us
    unnamed x7, local copies, waits for them, and re-layouts  3.21 us

profile of v5, /device:TPU:6, one launch (start us, length us, event | category | flops | bytes accessed | tf_op | source)
XLA Modules:
  0.0 123.8 jit_solution(8270203982533342867)
XLA Ops:
  0.6 119.9 %shard_map.94 = (bf16[128,2048]{1,0:T(8,128)(2,1)}, bf16[128,896]{1,0:T(8,128)(2,1)}, f32[896]{0:T(1024)}) custom-call(bf16[128,2048]{1,0:T(8,128)(2,1)} %bitcast.5, bf16[128,2048]{1,0:T(8,128)(2,1)} %bitcast.6, bf16[128,896]{1,0:T(8,128)(2,1)} %bitcast.8, f32[896]{0:T(1024)} %gain_ref.1, bf16[112,2,2048]{2,1,0:T(2,128)(2,1)} %kv_hbm.1, ...), custom_call_target="tpu_custom_call" | custom-call | tf_op jit(solution)/shard_map/pallas_call | solution.py:669
  120.6 0.0 copy-start
  120.6 1.9 %copy.13 = bf16[1,128,2048]{2,1,0:T(8,128)(2,1)} copy(bf16[1,128,2048]{2,1,0:T(8,128)(2,1)} %bitcast.7) | data formatting | bytes 1048576
  122.5 0.0 copy-done
  122.5 0.0 copy-start.1
  122.5 0.7 copy.14
  123.2 0.0 copy-done.1
  123.2 0.6 copy.15
Async XLA Ops:
  120.6 1.9 %copy-start = (bf16[128,896]{1,0:T(8,128)(2,1)S(1)}, bf16[128,896]{1,0:T(8,128)(2,1)}, u32[]{:S(2)}) copy-start(bf16[128,896]{1,0:T(8,128)(2,1)} %get-tuple-element.7) | copy-start | bytes 688132
  122.5 0.7 copy-start.1

commit v6 on v5

--- a/solution.py
+++ b/solution.py
@@ -600,7 +600,6 @@
 
     scatter(half - 1)
     scatter(half - 2)
-    scatter_rest()
     gain_one()
     fetch_sent()
     if half > 2:
@@ -610,8 +609,8 @@
     for way in range(2):
         pass_on(half, way, way).start()
     own[...] = added[:rows]
-    gather_rest()
     relay(half - 1, True)
+    scatter_rest()
     gain_two()
     heads = q_ref.shape[1] // HEAD_DIM
     turns = max(half - 3, 0)
@@ -632,6 +631,7 @@
     else:
         gain_three()
     gain_four()
+    gather_rest()
     if half > 2:
         relay(1, False)
 

time: 125 us -> 123 us (0.984)
  Pallas kernels: 120 us -> 118 us
    pallas_call x1, Pallas kernels: 120 us -> 118 us  [on_device(): pl.pallas_call(functools.partial(kernel, ny, nz, nb), out_shape=(jax.Shap...]
where the time goes in v6:
time: 123 us; the launch traced here: 122 us
  Pallas kernels  118 us (96%)
  local copies, waits for them, and re-layouts  3.21 us (3%)
    pallas_call x1, Pallas kernels, on_device(): pl.pallas_call(functools.partial(kernel, ny, nz, nb), out_shape=(jax.Shap...  118 us
    unnamed x7, local copies, waits for them, and re-layouts  3.21 us

profile of v6, /device:TPU:6, one launch (start us, length us, event | category | flops | bytes accessed | tf_op | source)
XLA Modules:
  0.0 122.2 jit_solution(17693918410287258426)
XLA Ops:
  0.6 118.4 %shard_map.94 = (bf16[128,2048]{1,0:T(8,128)(2,1)}, bf16[128,896]{1,0:T(8,128)(2,1)}, f32[896]{0:T(1024)}) custom-call(bf16[128,2048]{1,0:T(8,128)(2,1)} %bitcast.5, bf16[128,2048]{1,0:T(8,128)(2,1)} %bitcast.6, bf16[128,896]{1,0:T(8,128)(2,1)} %bitcast.8, f32[896]{0:T(1024)} %gain_ref.1, bf16[112,2,2048]{2,1,0:T(2,128)(2,1)} %kv_hbm.1, ...), custom_call_target="tpu_custom_call" | custom-call | tf_op jit(solution)/shard_map/pallas_call | solution.py:669
  119.0 0.0 copy-start
  119.0 1.9 %copy.13 = bf16[1,128,2048]{2,1,0:T(8,128)(2,1)} copy(bf16[1,128,2048]{2,1,0:T(8,128)(2,1)} %bitcast.7) | data formatting | bytes 1048576
  120.9 0.0 copy-done
  120.9 0.0 copy-start.1
  120.9 0.7 copy.14
  121.6 0.0 copy-done.1
  121.6 0.6 copy.15
Async XLA Ops:
  119.0 1.9 %copy-start = (bf16[128,896]{1,0:T(8,128)(2,1)S(1)}, bf16[128,896]{1,0:T(8,128)(2,1)}, u32[]{:S(2)}) copy-start(bf16[128,896]{1,0:T(8,128)(2,1)} %get-tuple-element.7) | copy-start | bytes 688132
  120.9 0.7 copy-start.1
